TPU v7x, 32 devices: a whole 2x2x4 slice. The times are simulated.
32 devices in a mesh: head: 4 (over x, core), blk: 8 (over z, y).
Axes of the slice: x: 2, y: 2, z: 4, core: 2. Of those that a mesh axis runs over, the one named last changes fastest.
Arguments:
- queries: bfloat16 [6144, 32, 128], P(('blk', 'head')), may hold values from -6 to 6
- rotated_keys: bfloat16 [6144, 8, 128], P(('blk', 'head')), may hold values from -6 to 6
- value_vectors: bfloat16 [6144, 8, 128], P(('blk', 'head')), may hold values from -6 to 6
- block_list: int32 [8, 48, 8], replicated, may hold values from 0 to 47, as said below
- grad_out: bfloat16 [6144, 32, 128], P(('blk', 'head')), may hold values from -6 to 6
Outputs:
- attn_out: bfloat16 [6144, 32, 128], P(('blk', 'head'))
- grad_queries: bfloat16 [6144, 32, 128], P(('blk', 'head'))
- key_gradient: bfloat16 [6144, 8, 128], P(('blk', 'head'))
- value_gradient: bfloat16 [6144, 8, 128], P(('blk', 'head'))
Inputs may be any that keep to these rules, and one draw needn't show every extreme that they name: Slot 0 of block_list[g, b, :] is b itself; every other slot names a distinct block below b or repeats b. For one head g, the blocks listed by the 6 query blocks of a run (blocks r * 6 to (r + 1) * 6 - 1) lie in that run or, for each earlier run, in one single block of it; the last query block of every run but the first lists a block of the run before.
All inputs are finite; a program needn't handle non-finite values.
Results may differ from a plain program's by a relative error of at most 0.035.
Values may be sent and summed in bfloat16 or wider, within the bound.
A program may use at most 192 MiB of HBM per device.

v0:
```python
import jax
import jax.numpy as jnp
from jax import lax
from jax.sharding import PartitionSpec as P

BLOCK_TOKENS = 128
TOPK = 8


def on_device(queries, rotated_keys, value_vectors, block_list, grad_out):
    query_h, key_h, value_h, grad_h = (
        lax.all_to_all(queries, "head", split_axis=1, concat_axis=0, tiled=True),
        lax.all_to_all(rotated_keys, "head", split_axis=1, concat_axis=0, tiled=True),
        lax.all_to_all(value_vectors, "head", split_axis=1, concat_axis=0, tiled=True),
        lax.all_to_all(grad_out, "head", split_axis=1, concat_axis=0, tiled=True),
    )
    run_len, head_count, head_width = query_h.shape
    groups = key_h.shape[1]
    group_width = head_count // groups
    block_ids = run_len // BLOCK_TOKENS
    peers = lax.axis_size("blk")
    rank = lax.axis_index("blk")
    head_rank = lax.axis_index("head")
    score_scale = head_width ** (-0.5)
    offsets = jnp.arange(BLOCK_TOKENS, dtype=jnp.int32)
    lists_here = lax.dynamic_slice_in_dim(block_list, head_rank * groups, groups, 0)
    lists_mine = lax.dynamic_slice_in_dim(lists_here, rank * block_ids, block_ids, 1)
    listing = lists_here.reshape(groups, peers, block_ids * TOPK)
    my_blocks = rank * block_ids + jnp.arange(block_ids, dtype=jnp.int32)
    present = jnp.any(listing[:, :, :, None] == my_blocks, axis=2)
    present = present & (jnp.arange(peers) != rank)[None, :, None]
    owner = lists_mine // block_ids
    target = jnp.where(owner == rank, peers + lists_mine % block_ids, owner)
    empty = jnp.zeros((groups, block_ids, TOPK, BLOCK_TOKENS, head_width), jnp.bfloat16)
    piece = (
        lax.all_gather(key_h, "blk", axis=0, tiled=True),
        lax.all_gather(value_h, "blk", axis=0, tiled=True),
    )
    rows = piece[0].shape[0]
    position = lists_mine[..., None] * BLOCK_TOKENS + offsets
    inside = ((position >= 0) & (position < rows))[..., None]
    safe = jnp.clip(position, 0, rows - 1)
    new_keys = jnp.stack([jnp.take(piece[0][:, g], safe[g], axis=0) for g in range(groups)])
    new_values = jnp.stack([jnp.take(piece[1][:, g], safe[g], axis=0) for g in range(groups)])
    picked_keys = jnp.where(inside, new_keys, empty)
    picked_values = jnp.where(inside, new_values, empty)
    items = groups * block_ids
    query_items = jnp.transpose(
        query_h.reshape(block_ids, BLOCK_TOKENS, groups, group_width, head_width), (2, 0, 1, 3, 4)
    ).reshape(items, BLOCK_TOKENS * group_width, head_width)
    grad_items = jnp.transpose(
        grad_h.reshape(block_ids, BLOCK_TOKENS, groups, group_width, head_width), (2, 0, 1, 3, 4)
    ).reshape(items, BLOCK_TOKENS * group_width, head_width)
    key_items = picked_keys.reshape(items, TOPK * BLOCK_TOKENS, head_width)
    value_items = picked_values.reshape(items, TOPK * BLOCK_TOKENS, head_width)
    slot_ids = jnp.arange(TOPK, dtype=jnp.int32)
    earlier = slot_ids[None, :] < slot_ids[:, None]
    repeated = jnp.any((lists_mine[..., :, None] == lists_mine[..., None, :]) & earlier, axis=-1)
    query_pos = my_blocks[:, None] * BLOCK_TOKENS + offsets
    key_pos = lists_mine[..., None] * BLOCK_TOKENS + offsets
    allowed = (key_pos[:, :, None, :, :] <= query_pos[None, :, :, None, None]) & jnp.logical_not(
        repeated
    )[:, :, None, :, None]
    allowed = allowed.reshape(items, BLOCK_TOKENS, TOPK * BLOCK_TOKENS)

    def attend(item):
        query_blk, grad_blk, key_blk, value_blk, allowed_blk = item
        scores = (
            jnp.einsum("rd,cd->rc", query_blk, key_blk, preferred_element_type=jnp.float32)
            * score_scale
        )
        scores = jnp.where(
            allowed_blk[:, None, :], scores.reshape(BLOCK_TOKENS, group_width, -1), -jnp.inf
        ).reshape(BLOCK_TOKENS * group_width, -1)
        row_max = jnp.max(scores, axis=-1, keepdims=True)
        log_total = row_max + jnp.log(jnp.sum(jnp.exp(scores - row_max), axis=-1, keepdims=True))
        probs = jnp.exp(scores - log_total)
        probs_b = probs.astype(jnp.bfloat16)
        output_b = jnp.dot(probs_b, value_blk, preferred_element_type=jnp.float32).astype(
            jnp.bfloat16
        )
        row_dot = jnp.sum(
            grad_blk.astype(jnp.float32) * output_b.astype(jnp.float32), axis=-1, keepdims=True
        )
        grad_probs = jnp.einsum(
            "rd,cd->rc", grad_blk, value_blk, preferred_element_type=jnp.float32
        )
        grad_scores_b = (probs * (grad_probs - row_dot)).astype(jnp.bfloat16)
        query_grad = (
            jnp.dot(grad_scores_b, key_blk, preferred_element_type=jnp.float32) * score_scale
        ).astype(jnp.bfloat16)
        key_slots = (
            jnp.einsum("rc,rd->cd", grad_scores_b, query_blk, preferred_element_type=jnp.float32)
            * score_scale
        )
        value_slots = jnp.einsum("rc,rd->cd", probs_b, grad_blk, preferred_element_type=jnp.float32)
        return (output_b, query_grad, key_slots, value_slots)

    outputs, query_grads, key_slots, value_slots = lax.map(
        attend, (query_items, grad_items, key_items, value_items, allowed)
    )

    def regroup(result):
        return jnp.transpose(
            result.reshape(groups, block_ids, BLOCK_TOKENS, group_width, head_width),
            (1, 2, 0, 3, 4),
        ).reshape(run_len, head_count, head_width)

    attn_h = regroup(outputs)
    query_grad_h = regroup(query_grads)
    target_flat = target.reshape(groups, block_ids * TOPK)
    to_peer = (target_flat[:, None, :] == jnp.arange(peers, dtype=jnp.int32)[None, :, None]).astype(
        jnp.bfloat16
    )
    to_local = (
        target_flat[:, None, :] == (peers + jnp.arange(block_ids, dtype=jnp.int32))[None, :, None]
    ).astype(jnp.bfloat16)

    def route(table, form, slots):
        upper = slots.astype(jnp.bfloat16)
        lower = (slots - upper.astype(jnp.float32)).astype(jnp.bfloat16)
        total = jnp.einsum(form, table, upper, preferred_element_type=jnp.float32)
        return total + jnp.einsum(form, table, lower, preferred_element_type=jnp.float32)

    def settle(slots):
        slots = slots.reshape(groups, block_ids * TOPK, BLOCK_TOKENS, head_width)
        remote = route(to_peer, "gje,gesd->jgsd", slots).astype(jnp.bfloat16)
        local = route(to_local, "gbe,gesd->bsgd", slots).astype(jnp.bfloat16)
        return (remote, local)

    remote_keys, local_keys_part = settle(key_slots)
    remote_values, local_values_part = settle(value_slots)
    back_keys, back_values = (
        lax.all_to_all(remote_keys, "blk", split_axis=0, concat_axis=0, tiled=True),
        lax.all_to_all(remote_values, "blk", split_axis=0, concat_axis=0, tiled=True),
    )
    marker_back = present.astype(jnp.bfloat16)

    def finish(local_part, arrived):
        total = lax.optimization_barrier(local_part).astype(jnp.float32)
        total = total + jnp.einsum(
            "gib,igsd->bsgd", marker_back, arrived, preferred_element_type=jnp.float32
        )
        return total.astype(jnp.bfloat16).reshape(run_len, groups, head_width)

    key_grad_h = finish(local_keys_part, back_keys)
    value_grad_h = finish(local_values_part, back_values)
    return (
        lax.all_to_all(attn_h, "head", split_axis=0, concat_axis=1, tiled=True),
        lax.all_to_all(query_grad_h, "head", split_axis=0, concat_axis=1, tiled=True),
        lax.all_to_all(key_grad_h, "head", split_axis=0, concat_axis=1, tiled=True),
        lax.all_to_all(value_grad_h, "head", split_axis=0, concat_axis=1, tiled=True),
    )


def solution(mesh):
    in_specs = (
        P(("blk", "head"), None, None),
        P(("blk", "head"), None, None),
        P(("blk", "head"), None, None),
        P(),
        P(("blk", "head"), None, None),
    )
    out_specs = (
        P(("blk", "head"), None, None),
        P(("blk", "head"), None, None),
        P(("blk", "head"), None, None),
        P(("blk", "head"), None, None),
    )
    return jax.shard_map(
        on_device, mesh=mesh, in_specs=in_specs, out_specs=out_specs, check_vma=False
    )
```

profile of v0, /device:TPU:13, one launch (start us, length us, event | category | flops | bytes accessed | tf_op | source)
XLA Modules:
  0.0 534.4 jit_solution(6253749279841626002)
XLA Ops:
  8.3 9.6 %all_to_all.148 = bf16[192,8,128]{2,0,1:T(8,128)(2,1)S(1)} all-to-all(bf16[192,8,128]{2,0,1:T(8,128)(2,1)S(1)} %copy.121), channel_id=1, replica_groups=mesh['head'=4,'blk'=8] {'head'}, dimensions={1} | all-to-all | bytes 786432 | tf_op jit(solution)/shard_map/all_to_all | solution.py:13
  18.9 9.8 %all_to_all.149 = bf16[192,8,128]{2,0,1:T(8,128)(2,1)S(1)} all-to-all(bf16[192,8,128]{2,0,1:T(8,128)(2,1)S(1)} %copy.123), channel_id=1, replica_groups=mesh['head'=4,'blk'=8] {'head'}, dimensions={1} | all-to-all | bytes 786432 | tf_op jit(solution)/shard_map/all_to_all | solution.py:14
  31.3 4.7 all-to-all-start
  39.0 16.3 %all-to-all-done = bf16[192,32,128]{2,0,1:T(8,128)(2,1)S(1)} async-done(((bf16[192,32,128]{2,0,1:T(8,128)(2,1)}), bf16[192,32,128]{2,0,1:T(8,128)(2,1)S(1)}, u32[]{:S(2)}, u32[]{:S(2)}) %all-to-all-start) | async-done | bytes 1572896 | tf_op jit(solution)/shard_map/all_to_all | solution.py:12
  64.7 14.3 %all-to-all-done.3 = bf16[192,32,128]{2,0,1:T(8,128)(2,1)S(1)} async-done(((bf16[192,32,128]{2,0,1:T(8,128)(2,1)}), bf16[192,32,128]{2,0,1:T(8,128)(2,1)S(1)}, u32[]{:S(2)}, u32[]{:S(2)}) %all-to-all-start.3) | async-done | bytes 1572896 | tf_op jit(solution)/shard_map/all_to_all | solution.py:15
  83.6 22.2 %gather_fusion = bf16[6144,128]{1,0:T(8,128)(2,1)} fusion(bf16[6144,128]{1,0:T(8,128)(2,1)S(1)} %get-tuple-element.156, s32[6144]{0:T(1024)S(1)} %get-tuple-element.160), kind=kCustom, calls=%fused_computation.clone | custom fusion | bytes 3170304 | tf_op jit(solution)/shard_map/jit(_take)/gather | solution.py:43
  105.8 33.8 %all-gather.5.cloned.1.call-done = bf16[6144,2,128]{2,0,1:T(8,128)(2,1)} async-done(((bf16[768,2,128]{2,0,1:T(8,128)(2,1)}), bf16[6144,2,128]{2,0,1:T(8,128)(2,1)}) %all-gather.5.cloned.1.call-update) | async-done | bytes 3145744 | tf_op jit(solution)/shard_map/all_gather | solution.py:37
  142.9 22.8 %gather_fusion.2 = bf16[6144,128]{1,0:T(8,128)(2,1)} fusion(bf16[6144,128]{1,0:T(8,128)(2,1)} %get-tuple-element.154, s32[6144]{0:T(1024)S(1)} %get-tuple-element.160), kind=kCustom, calls=%fused_computation.2.clone | custom fusion | bytes 3170304 | tf_op jit(solution)/shard_map/jit(_take)/gather | solution.py:44
  165.7 22.2 %gather_fusion.3 = bf16[6144,128]{1,0:T(8,128)(2,1)} fusion(bf16[6144,128]{1,0:T(8,128)(2,1)S(1)} %get-tuple-element.155, s32[6144]{0:T(1024)S(1)} %get-tuple-element.161), kind=kCustom, calls=%fused_computation.3.clone | custom fusion | bytes 3170304 | tf_op jit(solution)/shard_map/jit(_take)/gather | solution.py:44
  187.9 22.2 %gather_fusion.1 = bf16[6144,128]{1,0:T(8,128)(2,1)} fusion(bf16[6144,128]{1,0:T(8,128)(2,1)S(1)} %get-tuple-element.157, s32[6144]{0:T(1024)S(1)} %get-tuple-element.161), kind=kCustom, calls=%fused_computation.1.clone | custom fusion | bytes 3170304 | tf_op jit(solution)/shard_map/jit(_take)/gather | solution.py:43
  210.1 5.9 %select_bitcast_fusion = (bf16[1,6,8,128,128]{4,3,2,1,0:T(8,128)(2,1)S(1)}, bf16[1,6,8,128,128]{4,3,2,1,0:T(8,128)(2,1)S(1)}, bf16[1,6,8,128,128]{4,3,2,1,0:T(8,128)(2,1)S(1)}, bf16[1,6,8,128,128]{4,3,2,1,0:T(8,128)(2,1)S(1)}) fusion(bf16[6,8,128,128]{3,2,1,0:T(8,128)(2,1)} %bitcast.253, pred[6,8,128]{2,1,0:T(8,128)(4,1)S(1)} %get-tuple-element.159, ...), kind=kLoop, calls=%fused_computation.62 | loop fusion | flops 3145728 | bytes 12595200 | tf_op jit(solution)/shard_map/stack | solution.py:44
  216.6 5.1 broadcast_select_fusion
  221.8 185.2 %while.16 = (s32[]{:T(128)}, bf16[12,512,128]{2,1,0:T(8,128)(2,1)}, bf16[12,512,128]{2,1,0:T(8,128)(2,1)}, f32[12,1024,128]{2,1,0:T(8,128)}, f32[12,1024,128]{2,...) while((s32[]{:T(128)}, bf16[12,512,128]{2,1,0:T(8,128)(2,1)}, ...), condition=%wide.region_5.7_spmd, body=%wide.region_1.6_spmd.sunk | while | flops 812710912 | bytes 20212868 | solution.py:99
  407.0 6.3 %fusion.52 = f32[2,128,128,8]{2,3,1,0:T(8,128)S(1)} fusion(f32[2,48,128,128]{3,2,1,0:T(8,128)} %bitcast.232, s32[2,48]{1,0:T(2,128)S(1)} %eq.69), kind=kOutput, calls=%fused_computation.88 | convolution fusion | flops 31458048 | bytes 7340416 | tf_op jit(solution)/shard_map/gje,gesd->jgsd/dot_general | solution.py:123
  417.7 5.9 %all-to-all-start.8 = ((bf16[8,2,128,128]{3,2,1,0:T(8,128)(2,1)}), bf16[8,2,128,128]{3,2,1,0:T(8,128)(2,1)S(1)}, u32[]{:S(2)}, u32[]{:S(2)}) async-start(bf16[8,2,128,128]{3,2,1,0:T(8,128)(2,1)} %copy.150), calls=%async_computation.8 | async-start | bytes 1048576 | tf_op jit(solution)/shard_map/all_to_all | solution.py:135
  423.6 6.3 %fusion.50 = f32[2,128,128,8]{2,3,1,0:T(8,128)S(1)} fusion(f32[2,48,128,128]{3,2,1,0:T(8,128)} %bitcast.236, s32[2,48]{1,0:T(2,128)S(1)} %eq.69), kind=kOutput, calls=%fused_computation.86 | convolution fusion | flops 31458048 | bytes 7340416 | tf_op jit(solution)/shard_map/gje,gesd->jgsd/dot_general | solution.py:123
  436.3 6.3 %all-to-all-start.6 = ((bf16[8,2,128,128]{3,2,1,0:T(8,128)(2,1)}), bf16[8,2,128,128]{3,2,1,0:T(8,128)(2,1)S(1)}, u32[]{:S(2)}, u32[]{:S(2)}) async-start(bf16[8,2,128,128]{3,2,1,0:T(8,128)(2,1)} %copy.141), calls=%async_computation.6 | async-start | bytes 1048576 | tf_op jit(solution)/shard_map/all_to_all | solution.py:134
  445.2 9.4 %all-to-all-done.6 = bf16[8,2,128,128]{3,2,1,0:T(8,128)(2,1)S(1)} async-done(((bf16[8,2,128,128]{3,2,1,0:T(8,128)(2,1)}), bf16[8,2,128,128]{3,2,1,0:T(8,128)(2,1)S(1)}, u32[]{:S(2)}, u32[]{:S(2)}) %all-to-all-start.6) | async-done | bytes 524320 | tf_op jit(solution)/shard_map/all_to_all | solution.py:134
  454.6 4.9 all-to-all-start.4
  462.5 16.2 %all-to-all-done.4 = bf16[768,8,128]{2,1,0:T(8,128)(2,1)} async-done(((bf16[768,8,128]{2,1,0:T(8,128)(2,1)}), bf16[768,8,128]{2,1,0:T(8,128)(2,1)}, u32[]{:S(2)}, u32[]{:S(2)}) %all-to-all-start.4) | async-done | bytes 1572896 | tf_op jit(solution)/shard_map/all_to_all | solution.py:149
  478.8 5.5 %all-to-all-start.5 = ((bf16[768,8,128]{2,1,0:T(8,128)(2,1)}), bf16[768,8,128]{2,1,0:T(8,128)(2,1)}, u32[]{:S(2)}, u32[]{:S(2)}) async-start(bf16[768,8,128]{2,1,0:T(8,128)(2,1)} %copy.136), calls=%async_computation.5 | async-start | bytes 3145728 | tf_op jit(solution)/shard_map/all_to_all | solution.py:150
  484.3 6.3 %fusion.53 = f32[2,128,128,6]{2,3,1,0:T(8,128)S(1)} fusion(f32[2,48,128,128]{3,2,1,0:T(8,128)} %bitcast.233, s32[2,48]{1,0:T(2,128)S(1)} %eq.69, s32[6]{0:T(128)S(1)} %iota_add_fusion.1), kind=kOutput, calls=%fused_computation.89 | convolution fusion | flops 25166400 | bytes 7078296 | tf_op jit(solution)/shard_map/gbe,gesd->bsgd/dot_general | solution.py:123
  490.6 6.2 %fusion.44 = bf16[6,128,2,128]{3,0,1,2:T(8,128)(2,1)S(1)} fusion(f32[2,128,128,6]{2,3,1,0:T(8,128)S(1)} %fusion.53, f32[2,48,128,128]{3,2,1,0:T(8,128)} %bitcast.234, s32[2,48]{1,0:T(2,128)S(1)} %eq.69, s32[6]{0:T(128)S(1)} %iota_add_fusion.1), kind=kOutput, calls=%fused_computation.80 | convolution fusion | flops 19268160 | bytes 7471512 | tf_op jit(solution)/shard_map/gbe,gesd->bsgd/dot_general | solution.py:122
  508.1 6.3 %fusion.46 = bf16[6,128,2,128]{3,0,1,2:T(8,128)(2,1)S(1)} fusion(f32[2,128,128,6]{2,3,1,0:T(8,128)S(1)} %fusion.51, f32[2,48,128,128]{3,2,1,0:T(8,128)} %bitcast.237, s32[2,48]{1,0:T(2,128)S(1)} %eq.69, s32[6]{0:T(128)S(1)} %iota_add_fusion.1), kind=kOutput, calls=%fused_computation.82 | convolution fusion | flops 19268160 | bytes 7471512 | tf_op jit(solution)/shard_map/gbe,gesd->bsgd/dot_general | solution.py:122
  (296 shorter events, 249.9 us)
Async XLA Ops:
  7.2 11.6 %copy-start.11 = (bf16[192,8,128]{2,1,0:T(8,128)(2,1)S(1)}, bf16[192,8,128]{2,1,0:T(8,128)(2,1)}, u32[]{:S(2)}) copy-start(bf16[192,8,128]{2,1,0:T(8,128)(2,1)} %param.11) | copy-start | bytes 1179652
  7.2 74.3 %all-gather.3.cloned.1.call-start = ((), (), s32[]{:S(2)}) async-start(), calls=%async_computation.10 | async-start | bytes 3538944 | tf_op jit(solution)/shard_map/all_gather | solution.py:36
  18.0 11.6 %copy-start.7 = (bf16[192,32,128]{2,1,0:T(8,128)(2,1)S(1)}, bf16[192,32,128]{2,1,0:T(8,128)(2,1)}, u32[]{:S(2)}) copy-start(bf16[192,32,128]{2,1,0:T(8,128)(2,1)} %param.9) | copy-start | bytes 4718596
  18.8 120.8 %all-gather.5.cloned.1.call-start = ((), (), s32[]{:S(2)}) async-start(), calls=%async_computation.11 | async-start | bytes 3538944 | tf_op jit(solution)/shard_map/all_gather | solution.py:37
  31.3 4.8 copy-start.12
  31.3 5.9 %copy-start.8 = (bf16[192,32,128]{2,1,0:T(8,128)(2,1)S(1)}, bf16[192,32,128]{2,1,0:T(8,128)(2,1)}, u32[]{:S(2)}) copy-start(bf16[192,32,128]{2,1,0:T(8,128)(2,1)} %param.13) | copy-start | bytes 4718596
  31.3 24.0 %all-to-all-start = ((bf16[192,32,128]{2,0,1:T(8,128)(2,1)}), bf16[192,32,128]{2,0,1:T(8,128)(2,1)S(1)}, u32[]{:S(2)}, u32[]{:S(2)}) async-start(bf16[192,32,128]{2,0,1:T(8,128)(2,1)} %copy.117), calls=%async_computation | async-start | bytes 3145728 | tf_op jit(solution)/shard_map/all_to_all | solution.py:12
  55.3 23.7 %all-to-all-start.3 = ((bf16[192,32,128]{2,0,1:T(8,128)(2,1)}), bf16[192,32,128]{2,0,1:T(8,128)(2,1)S(1)}, u32[]{:S(2)}, u32[]{:S(2)}) async-start(bf16[192,32,128]{2,0,1:T(8,128)(2,1)} %copy.125), calls=%async_computation.3 | async-start | bytes 3145728 | tf_op jit(solution)/shard_map/all_to_all | solution.py:15
  187.9 22.2 %copy-start.2 = (bf16[6144,128]{1,0:T(8,128)(2,1)S(1)}, bf16[6144,128]{1,0:T(8,128)(2,1)}, u32[]{:S(2)}) copy-start(bf16[6144,128]{1,0:T(8,128)(2,1)} %gather_fusion) | copy-start | bytes 4718596
  407.0 6.3 %copy-start = (f32[12,1024,128]{2,1,0:T(8,128)S(1)}, f32[12,1024,128]{2,1,0:T(8,128)}, u32[]{:S(2)}) copy-start(f32[12,1024,128]{2,1,0:T(8,128)} %get-tuple-element.63) | copy-start | bytes 18874372
  417.7 17.8 %all-to-all-start.8 = ((bf16[8,2,128,128]{3,2,1,0:T(8,128)(2,1)}), bf16[8,2,128,128]{3,2,1,0:T(8,128)(2,1)S(1)}, u32[]{:S(2)}, u32[]{:S(2)}) async-start(bf16[8,2,128,128]{3,2,1,0:T(8,128)(2,1)} %copy.150), calls=%async_computation.8 | async-start | bytes 1048576 | tf_op jit(solution)/shard_map/all_to_all | solution.py:135
  423.6 6.3 %copy-start.1 = (f32[12,1024,128]{2,1,0:T(8,128)S(1)}, f32[12,1024,128]{2,1,0:T(8,128)}, u32[]{:S(2)}) copy-start(f32[12,1024,128]{2,1,0:T(8,128)} %get-tuple-element.62) | copy-start | bytes 18874372
  433.4 9.2 %copy-start.10 = (bf16[12,512,128]{2,1,0:T(8,128)(2,1)S(1)}, bf16[12,512,128]{2,1,0:T(8,128)(2,1)}, u32[]{:S(2)}) copy-start(bf16[12,512,128]{2,1,0:T(8,128)(2,1)} %get-tuple-element.60) | copy-start | bytes 4718596
  436.3 18.3 %all-to-all-start.6 = ((bf16[8,2,128,128]{3,2,1,0:T(8,128)(2,1)}), bf16[8,2,128,128]{3,2,1,0:T(8,128)(2,1)S(1)}, u32[]{:S(2)}, u32[]{:S(2)}) async-start(bf16[8,2,128,128]{3,2,1,0:T(8,128)(2,1)} %copy.141), calls=%async_computation.6 | async-start | bytes 1048576 | tf_op jit(solution)/shard_map/all_to_all | solution.py:134
  445.2 14.8 %copy-start.9 = (bf16[12,512,128]{2,1,0:T(8,128)(2,1)S(1)}, bf16[12,512,128]{2,1,0:T(8,128)(2,1)}, u32[]{:S(2)}) copy-start(bf16[12,512,128]{2,1,0:T(8,128)(2,1)} %get-tuple-element.61) | copy-start | bytes 4718596
  454.6 5.8 %copy-start.3 = (bf16[8,2,128,128]{3,2,1,0:T(8,128)(2,1)}, bf16[8,2,128,128]{3,2,1,0:T(8,128)(2,1)S(1)}, u32[]{:S(2)}) copy-start(bf16[8,2,128,128]{3,2,1,0:T(8,128)(2,1)S(1)} %all-to-all-done.6) | copy-start | bytes 1572868
  454.6 24.2 %all-to-all-start.4 = ((bf16[768,8,128]{2,1,0:T(8,128)(2,1)}), bf16[768,8,128]{2,1,0:T(8,128)(2,1)}, u32[]{:S(2)}, u32[]{:S(2)}) async-start(bf16[768,8,128]{2,1,0:T(8,128)(2,1)} %copy.133), calls=%async_computation.4 | async-start | bytes 3145728 | tf_op jit(solution)/shard_map/all_to_all | solution.py:149
  478.8 18.1 %slice-start = ((s8[6291456]{0:T(1024)(128)(4,1)}), s8[2097152]{0:T(1024)(128)(4,1)S(1)}, s32[]{:S(2)}) async-start(s8[6291456]{0:T(1024)(128)(4,1)} %bitcast.239), calls=%async_computation.12 | async-start | bytes 4194304
  478.8 24.8 %all-to-all-start.5 = ((bf16[768,8,128]{2,1,0:T(8,128)(2,1)}), bf16[768,8,128]{2,1,0:T(8,128)(2,1)}, u32[]{:S(2)}, u32[]{:S(2)}) async-start(bf16[768,8,128]{2,1,0:T(8,128)(2,1)} %copy.136), calls=%async_computation.5 | async-start | bytes 3145728 | tf_op jit(solution)/shard_map/all_to_all | solution.py:150
  484.3 12.6 %slice-start.1 = ((s8[6291456]{0:T(1024)(128)(4,1)}), s8[4194304]{0:T(1024)(128)(4,1)S(1)}, s32[]{:S(2)}) async-start(s8[6291456]{0:T(1024)(128)(4,1)} %bitcast.239), calls=%async_computation.13 | async-start | bytes 8388608
  496.9 3.4 copy-start.6
  503.5 12.5 %all-to-all-start.9 = ((bf16[768,2,128]{2,1,0:T(2,128)(2,1)}), bf16[768,2,128]{2,1,0:T(2,128)(2,1)S(1)}, u32[]{:S(2)}, u32[]{:S(2)}) async-start(bf16[768,2,128]{2,1,0:T(2,128)(2,1)} %copy.153), calls=%async_computation.9 | async-start | bytes 786432 | tf_op jit(solution)/shard_map/all_to_all | solution.py:152
  508.1 6.3 %copy-start.4 = (bf16[8,2,128,128]{3,2,1,0:T(8,128)(2,1)S(1)}, bf16[8,2,128,128]{3,2,1,0:T(8,128)(2,1)}, u32[]{:S(2)}) copy-start(bf16[8,2,128,128]{3,2,1,0:T(8,128)(2,1)} %copy-done.3) | copy-start | bytes 1572868
  516.0 10.2 %all-to-all-start.7 = ((bf16[768,2,128]{2,1,0:T(2,128)(2,1)}), bf16[768,2,128]{2,1,0:T(2,128)(2,1)S(1)}, u32[]{:S(2)}, u32[]{:S(2)}) async-start(bf16[768,2,128]{2,1,0:T(2,128)(2,1)} %copy.145), calls=%async_computation.7 | async-start | bytes 786432 | tf_op jit(solution)/shard_map/all_to_all | solution.py:151
  (1 other events, 0.8 us)
Sparse Core Ops, SparseCore 0:
  18.9 58.8 all-gather.2
  80.5 59.0 all-gather.4
where the time goes:
time: 544 us; the launch traced here: 534 us
  matrix products  177 us (33%)
  local copies, waits for them, and re-layouts  169 us (31%)
  waiting for transfers between devices  92.9 us (17%)
  starting transfers between devices  39.9 us (7%)
  other arithmetic  20.8 us (4%)
  blocking collectives  19.5 us (4%)
  between operations  14.7 us (3%)
    gather x2, local copies, waits for them, and re-layouts, on_device(): jnp.take(piece[1][:, g], safe[g], axis=0)  45 us
    gather x2, local copies, waits for them, and re-layouts, on_device(): jnp.take(piece[0][:, g], safe[g], axis=0)  44.4 us
    all_gather x1, waiting for transfers between devices, on_device(): lax.all_gather(value_h, 'blk', axis=0, tiled=True)  33.8 us
    dot_general x12, matrix products, attend(): jnp.einsum('rc,rd->cd', probs_b, grad_blk, preferred_element_type=jnp.flo...  27.6 us
    dot_general x12, matrix products, attend(): jnp.einsum('rc,rd->cd', grad_scores_b, query_blk, preferred_element_type=...  26.1 us
    dot_general x12, matrix products, attend(): jnp.dot(grad_scores_b, key_blk, preferred_element_type=jnp.float32)  24.6 us
    broadcast_in_dim x36, local copies, waits for them, and re-layouts, attend(): jnp.where(allowed_blk[:, None, :], scores.reshape(BLOCK_TOKENS, group_wid...  22.6 us
    dot_general x4, matrix products, route(): jnp.einsum(form, table, lower, preferred_element_type=jnp.float32)  22.4 us
  transfers between devices with their start and end apart: 10, of which 7 were waited for; matrix products, arithmetic and copies ran while one was open for 16% of the time, Pallas kernels for 0%

commit v1 on v0

v1 whole, which is shorter than its diff:
```python
import functools

import jax
import jax.numpy as jnp
from jax import lax
from jax.experimental import pallas as pl
from jax.experimental.pallas import tpu as pltpu
from jax.sharding import PartitionSpec as P

BLOCK = 128
TOPK = 8
LOG2E = 1.4426950408889634
MESH = pl.DeviceIdType.MESH
VMEM_LIMIT = 56 * 1024 * 1024


def greet(heads, peers):
    me = lax.axis_index("head")
    rank = lax.axis_index("blk")
    barrier = pltpu.get_barrier_semaphore()
    for d in range(1, heads):
        pl.semaphore_signal(
            barrier, inc=1, device_id=(lax.rem(me + d, heads), rank), device_id_type=MESH
        )
    for d in range(1, peers):
        pl.semaphore_signal(
            barrier, inc=1, device_id=(me, lax.rem(rank + d, peers)), device_id_type=MESH
        )
    pl.semaphore_wait(barrier, heads + peers - 2)
    return me, rank


def bring_kernel(
    heads, peers, groups, run_blocks,
    named, q_ref, do_ref, k_ref, v_ref,
    qh_ref, doh_ref, kv_ref, recv_ref,
    stage, own_sem, head_send, head_recv, blk_send, blk_recv,
):
    me, rank = greet(heads, peers)
    tokens = k_ref.shape[1]
    rows = q_ref.shape[1]

    def pieces(dest):
        part = pl.ds(dest * groups, groups)
        return (
            (k_ref.at[part], kv_ref.at[0, :, pl.ds(pl.multiple_of(me * tokens, 64), tokens)]),
            (v_ref.at[part], kv_ref.at[1, :, pl.ds(pl.multiple_of(me * tokens, 64), tokens)]),
            (q_ref.at[part], qh_ref.at[:, pl.ds(pl.multiple_of(me * rows, 128), rows)]),
            (do_ref.at[part], doh_ref.at[:, pl.ds(pl.multiple_of(me * rows, 128), rows)]),
        )

    remote = {}
    local = []
    for n in range(4):
        for d in range(1, heads):
            dest = lax.rem(me + d, heads)
            src, dst = pieces(dest)[n]
            copy = pltpu.make_async_remote_copy(
                src_ref=src, dst_ref=dst,
                send_sem=head_send.at[n, d], recv_sem=head_recv.at[n, d],
                device_id=(dest, rank), device_id_type=MESH,
            )
            copy.start()
            remote[n, d] = copy
        src, dst = pieces(me)[n]
        copy = pltpu.make_async_copy(src, dst, own_sem.at[n])
        copy.start()
        local.append(copy)
    for n in range(2):
        local[n].wait()
        for d in range(1, heads):
            remote[n, d].wait_recv()
    blk_copies = []
    for d in range(1, peers):
        peer = lax.rem(rank + d, peers)
        for g in range(groups):
            block = named[g * peers + peer]
            for n in range(2):
                total = jnp.zeros((BLOCK, kv_ref.shape[-1]), jnp.float32)
                for i in range(run_blocks):
                    weight = (block == i).astype(jnp.float32)
                    piece = kv_ref[n, g, i * BLOCK : (i + 1) * BLOCK, :]
                    total = total + weight * piece.astype(jnp.float32)
                stage[d, n, g] = total.astype(jnp.bfloat16)
        copy = pltpu.make_async_remote_copy(
            src_ref=stage.at[d], dst_ref=recv_ref.at[rank],
            send_sem=blk_send.at[d], recv_sem=blk_recv.at[d],
            device_id=(me, peer), device_id_type=MESH,
        )
        copy.start()
        blk_copies.append(copy)
    for n in range(2, 4):
        local[n].wait()
        for d in range(1, heads):
            remote[n, d].wait_recv()
    for copy in remote.values():
        copy.wait_send()
    for copy in blk_copies:
        copy.wait()


def attend_kernel(
    run_blocks, seq_blocks,
    place, lists, q_ref, do_ref, kv_ref, recv_ref,
    out_ref, dq_ref, own_ref, far_ref,
    k_buf, v_buf, acc_own, acc_far,
):
    g, b = pl.program_id(0), pl.program_id(1)
    groups = pl.num_programs(0)
    base = place[1] * run_blocks
    scale = q_ref.shape[-1] ** -0.5
    width = q_ref.shape[1] // BLOCK

    @pl.when(b == 0)
    def _():
        acc_own[...] = jnp.zeros_like(acc_own)
        acc_far[...] = jnp.zeros_like(acc_far)

    first = ((place[0] * groups + g) * seq_blocks + base + b) * TOPK
    slots = []
    for s in range(TOPK):
        listed = lists[first + s]
        mine = listed >= base
        at = jnp.clip(listed - base, 0, run_blocks - 1)
        owner = listed // run_blocks
        slots.append((listed, mine, at, owner))

        @pl.when(mine)
        def _():
            rows = pl.ds(pl.multiple_of(at * BLOCK, BLOCK), BLOCK)
            k_buf[s * BLOCK : (s + 1) * BLOCK] = kv_ref[0, g, rows, :]
            v_buf[s * BLOCK : (s + 1) * BLOCK] = kv_ref[1, g, rows, :]

        @pl.when(jnp.logical_not(mine))
        def _():
            k_buf[s * BLOCK : (s + 1) * BLOCK] = recv_ref[owner, 0, g]
            v_buf[s * BLOCK : (s + 1) * BLOCK] = recv_ref[owner, 1, g]

    q, do = q_ref[0], do_ref[0]
    keys, values = k_buf[...], v_buf[...]
    across = (((1,), (1,)), ((), ()))
    f32 = jnp.float32
    scores = lax.dot_general(keys, q, across, preferred_element_type=f32)
    shape = (BLOCK, q.shape[0])
    causal = lax.broadcasted_iota(jnp.int32, shape, 0) * width <= lax.broadcasted_iota(
        jnp.int32, shape, 1
    )
    parts = [jnp.where(causal, scores[:BLOCK], -1e30)]
    for s in range(1, TOPK):
        parts.append(
            jnp.where(slots[s][0] != base + b, scores[s * BLOCK : (s + 1) * BLOCK], -1e30)
        )
    scores = jnp.concatenate(parts, axis=0)
    top = jnp.max(scores, axis=0, keepdims=True)
    weights = jnp.exp2((scores - top) * (scale * LOG2E))
    probs = weights * (1.0 / jnp.sum(weights, axis=0, keepdims=True))
    probs_b = probs.astype(jnp.bfloat16)
    out_t = lax.dot_general(values.T, probs_b, (((1,), (0,)), ((), ())), preferred_element_type=f32)
    out_b = out_t.T.astype(jnp.bfloat16)
    out_ref[0] = out_b
    row_dot = jnp.sum(
        do.astype(f32).T * out_t.astype(jnp.bfloat16).astype(f32), axis=0, keepdims=True
    )
    grad_probs = lax.dot_general(values, do, across, preferred_element_type=f32)
    grad_scores = (probs * (grad_probs - row_dot)).astype(jnp.bfloat16)
    dq_t = lax.dot_general(
        keys.T, grad_scores, (((1,), (0,)), ((), ())), preferred_element_type=f32
    )
    dq_ref[0] = (dq_t * scale).T.astype(jnp.bfloat16)
    dk = jnp.dot(grad_scores, q, preferred_element_type=f32)
    dv = jnp.dot(probs_b, do, preferred_element_type=f32)
    for s in range(TOPK):
        listed, mine, at, owner = slots[s]
        dk_s, dv_s = dk[s * BLOCK : (s + 1) * BLOCK], dv[s * BLOCK : (s + 1) * BLOCK]

        @pl.when(mine)
        def _():
            rows = pl.ds(pl.multiple_of(at * BLOCK, BLOCK), BLOCK)
            acc_own[0, rows, :] += dk_s
            acc_own[1, rows, :] += dv_s

        @pl.when(jnp.logical_not(mine))
        def _():
            acc_far[owner, 0] += dk_s
            acc_far[owner, 1] += dv_s

    @pl.when(b == run_blocks - 1)
    def _():
        own_ref[0, 0] = (acc_own[0] * scale).astype(jnp.bfloat16)
        own_ref[1, 0] = acc_own[1].astype(jnp.bfloat16)
        for j in range(acc_far.shape[0]):
            far_ref[j, 0, 0] = (acc_far[j, 0] * scale).astype(jnp.bfloat16)
            far_ref[j, 1, 0] = acc_far[j, 1].astype(jnp.bfloat16)


def return_kernel(
    heads, peers, groups, run_blocks,
    named, outh_ref, dqh_ref, own_ref, far_ref,
    out_ref, dq_ref, kv_ref,
    recv, stage, own_sem, head_send, head_recv, blk_send, blk_recv,
):
    me, rank = greet(heads, peers)
    rows = out_ref.shape[1]
    tokens = kv_ref.shape[2]
    blk_copies = []
    for d in range(1, peers):
        peer = lax.rem(rank + d, peers)
        copy = pltpu.make_async_remote_copy(
            src_ref=far_ref.at[peer], dst_ref=recv.at[rank],
            send_sem=blk_send.at[d], recv_sem=blk_recv.at[d],
            device_id=(me, peer), device_id_type=MESH,
        )
        copy.start()
        blk_copies.append(copy)

    def pieces(dest):
        part = pl.ds(me * groups, groups)
        here = pl.ds(pl.multiple_of(dest * rows, 128), rows)
        some = pl.ds(pl.multiple_of(dest * tokens, 64), tokens)
        return (
            (outh_ref.at[:, here], out_ref.at[part]),
            (dqh_ref.at[:, here], dq_ref.at[part]),
            (stage.at[:, :, some], kv_ref.at[:, part]),
        )

    copies = []

    def send(n):
        for d in range(1, heads):
            dest = lax.rem(me + d, heads)
            src, dst = pieces(dest)[n]
            copy = pltpu.make_async_remote_copy(
                src_ref=src, dst_ref=dst,
                send_sem=head_send.at[n, d], recv_sem=head_recv.at[n, d],
                device_id=(dest, rank), device_id_type=MESH,
            )
            copy.start()
            copies.append(copy)
        src, dst = pieces(me)[n]
        copy = pltpu.make_async_copy(src, dst, own_sem.at[n])
        copy.start()
        copies.append(copy)

    send(0)
    send(1)
    for copy in blk_copies:
        copy.wait()
    for g in range(groups):
        for n in range(2):
            def settle(i, _):
                at = pl.ds(pl.multiple_of(i * BLOCK, BLOCK), BLOCK)

                def add(d, total):
                    peer = lax.rem(rank + d, peers)
                    weight = (named[g * peers + peer] == i).astype(jnp.float32)
                    return total + weight * recv[peer, n, g].astype(jnp.float32)

                total = own_ref[n, g, at, :].astype(jnp.float32)
                total = lax.fori_loop(1, peers, add, total)
                stage[n, g, at, :] = total.astype(jnp.bfloat16)
                return 0

            lax.fori_loop(0, run_blocks, settle, 0)
    send(2)
    for copy in copies:
        copy.wait()


def on_device(queries, rotated_keys, value_vectors, block_list, grad_out):
    tokens, head_count, width = queries.shape
    group_count = rotated_keys.shape[1]
    per_group = head_count // group_count
    heads, peers = lax.axis_size("head"), lax.axis_size("blk")
    me, rank = lax.axis_index("head"), lax.axis_index("blk")
    groups = group_count // heads
    run_len = tokens * heads
    run_blocks = run_len // BLOCK
    seq_blocks = block_list.shape[1]
    rows = tokens * per_group
    bf16 = jnp.bfloat16

    def by_group(array):
        array = array.reshape(tokens, group_count, -1, width)
        return jnp.transpose(array, (1, 0, 2, 3)).reshape(group_count, -1, width)

    lists_here = lax.dynamic_slice_in_dim(block_list, me * groups, groups, 0)
    listing = lists_here.reshape(groups, peers, run_blocks * TOPK)
    inside = (listing // run_blocks == rank) & (jnp.arange(peers) != rank)[None, :, None]
    named = jnp.max(jnp.where(inside, listing - rank * run_blocks, -1), axis=2).reshape(-1)

    any_space = pl.BlockSpec(memory_space=pl.ANY)
    vmem = pl.BlockSpec(memory_space=pltpu.VMEM)
    smem = pl.BlockSpec(memory_space=pltpu.SMEM)
    dma = pltpu.SemaphoreType.DMA
    params = functools.partial(
        pltpu.CompilerParams, has_side_effects=True, vmem_limit_bytes=VMEM_LIMIT
    )
    far_shape = (peers, 2, groups, BLOCK, width)
    own_shape = (2, groups, run_len, width)
    q_shape = (groups, rows * heads, width)
    qh, doh, kv, recv = pl.pallas_call(
        functools.partial(bring_kernel, heads, peers, groups, run_blocks),
        out_shape=(
            jax.ShapeDtypeStruct(q_shape, bf16),
            jax.ShapeDtypeStruct(q_shape, bf16),
            jax.ShapeDtypeStruct(own_shape, bf16),
            jax.ShapeDtypeStruct(far_shape, bf16),
        ),
        in_specs=[smem] + [any_space] * 4,
        out_specs=(any_space, any_space, vmem, any_space),
        scratch_shapes=[
            pltpu.VMEM(far_shape, bf16),
            dma((4,)), dma((4, heads)), dma((4, heads)), dma((peers,)), dma((peers,)),
        ],
        compiler_params=params(collective_id=0),
        name="bring",
    )(named, by_group(queries), by_group(grad_out), by_group(rotated_keys), by_group(value_vectors))

    place = jnp.stack([me, rank]).astype(jnp.int32)
    item = pl.BlockSpec((1, BLOCK * per_group, width), lambda g, b, *_: (g, b, 0))
    outh, dqh, own, far = pl.pallas_call(
        functools.partial(attend_kernel, run_blocks, seq_blocks),
        grid_spec=pltpu.PrefetchScalarGridSpec(
            num_scalar_prefetch=2,
            grid=(groups, run_blocks),
            in_specs=[
                item, item,
                pl.BlockSpec(own_shape, lambda g, b, *_: (0, 0, 0, 0)),
                pl.BlockSpec(far_shape, lambda g, b, *_: (0, 0, 0, 0, 0)),
            ],
            out_specs=(
                item, item,
                pl.BlockSpec((2, 1, run_len, width), lambda g, b, *_: (0, g, 0, 0)),
                pl.BlockSpec((peers, 2, 1, BLOCK, width), lambda g, b, *_: (0, 0, g, 0, 0)),
            ),
            scratch_shapes=[
                pltpu.VMEM((TOPK * BLOCK, width), bf16),
                pltpu.VMEM((TOPK * BLOCK, width), bf16),
                pltpu.VMEM((2, run_len, width), jnp.float32),
                pltpu.VMEM((peers, 2, BLOCK, width), jnp.float32),
            ],
        ),
        out_shape=(
            jax.ShapeDtypeStruct(q_shape, bf16),
            jax.ShapeDtypeStruct(q_shape, bf16),
            jax.ShapeDtypeStruct(own_shape, bf16),
            jax.ShapeDtypeStruct(far_shape, bf16),
        ),
        compiler_params=pltpu.CompilerParams(
            dimension_semantics=("arbitrary", "arbitrary"), vmem_limit_bytes=VMEM_LIMIT
        ),
        name="attend",
    )(place, block_list.reshape(-1), qh, doh, kv, recv)

    out_g, dq_g, kv_g = pl.pallas_call(
        functools.partial(return_kernel, heads, peers, groups, run_blocks),
        out_shape=(
            jax.ShapeDtypeStruct((group_count, rows, width), bf16),
            jax.ShapeDtypeStruct((group_count, rows, width), bf16),
            jax.ShapeDtypeStruct((2, group_count, tokens, width), bf16),
        ),
        in_specs=[smem, any_space, any_space, vmem, any_space],
        out_specs=(any_space, any_space, any_space),
        scratch_shapes=[
            pltpu.VMEM(far_shape, bf16),
            pltpu.VMEM(own_shape, bf16),
            dma((3,)), dma((3, heads)), dma((3, heads)), dma((peers,)), dma((peers,)),
        ],
        compiler_params=params(collective_id=1),
        name="give_back",
    )(named, outh, dqh, own, far)

    def by_token(array, count):
        array = array.reshape(group_count, tokens, count, width)
        return jnp.transpose(array, (1, 0, 2, 3)).reshape(tokens, group_count * count, width)

    return (
        by_token(out_g, per_group),
        by_token(dq_g, per_group),
        by_token(kv_g[0], 1),
        by_token(kv_g[1], 1),
    )


def solution(mesh):
    split = P(("blk", "head"), None, None)
    return jax.shard_map(
        on_device,
        mesh=mesh,
        in_specs=(split, split, split, P(), split),
        out_specs=(split, split, split, split),
        check_vma=False,
    )
```

time: 544 us -> 151 us (0.28); the launches traced: 534 us -> 148 us
  matrix products: 177 us -> 0 us
  local copies, waits for them, and re-layouts: 169 us -> 15 us
  Pallas kernels: 0 us -> 131 us
  waiting for transfers between devices: 92.9 us -> 0 us
  starting transfers between devices: 39.9 us -> 0 us
  blocking collectives: 19.5 us -> 0 us
  other arithmetic: 20.8 us -> 1.5 us
  between operations: 14.7 us -> 0.7 us
    dot_general x82 -> x0, matrix products: 177 us -> none  [the longest x12 27.6 us: attend(): jnp.einsum('rc,rd->cd', probs_b, grad_blk, preferred_element_type=jnp.flo...]
    pallas_call x0 -> x3, Pallas kernels: none -> 131 us  [the longest x1 49.1 us: on_device(): pl.pallas_call(functools.partial(bring_kernel, heads, peers, groups, run_...]
    gather x4 -> x0, local copies, waits for them, and re-layouts: 89.5 us -> none  [the longest x2 45 us: on_device(): jnp.take(piece[1][:, g], safe[g], axis=0)]
    all_to_all x8 -> x0, waiting for transfers between devices: 59 us -> none  [the longest x1 16.3 us: on_device(): lax.all_to_all(queries, 'head', split_axis=1, concat_axis=0, tiled=True)]
    all_to_all x8 -> x0, starting transfers between devices: 39.8 us -> none  [the longest x1 6.35 us: on_device(): lax.all_to_all(remote_keys, 'blk', split_axis=0, concat_axis=0, tiled=True)]
    all_gather x2 -> x0, waiting for transfers between devices: 33.8 us -> none  [the longest x1 33.8 us: on_device(): lax.all_gather(value_h, 'blk', axis=0, tiled=True)]
    broadcast_in_dim x36 -> x0, local copies, waits for them, and re-layouts: 22.6 us -> none  [attend(): jnp.where(allowed_blk[:, None, :], scores.reshape(BLOCK_TOKENS, group_wid...]
    all_to_all x2 -> x0, blocking collectives: 19.5 us -> none  [the longest x1 9.84 us: on_device(): lax.all_to_all(value_vectors, 'head', split_axis=1, concat_axis=0, tiled=...]
  transfers between devices with their start and end apart: 10 -> 0, of which waited for: 7 -> 0; matrix products, arithmetic and copies ran while one was open for 16% -> 0% of each run, Pallas kernels for 0% -> 0%
where the time goes in v1:
time: 151 us; the launch traced here: 148 us
  Pallas kernels  131 us (87%)
  local copies, waits for them, and re-layouts  15 us (10%)
    pallas_call x1, Pallas kernels, on_device(): pl.pallas_call(functools.partial(bring_kernel, heads, peers, groups, run_...  49.1 us
    pallas_call x1, Pallas kernels, on_device(): pl.pallas_call(functools.partial(return_kernel, heads, peers, groups, run...  47.2 us
    pallas_call x1, Pallas kernels, on_device(): pl.pallas_call(functools.partial(attend_kernel, run_blocks, seq_blocks),...  34.8 us
    transpose x2, local copies, waits for them, and re-layouts, by_token(): jnp.transpose(array, (1, 0, 2, 3))  4.89 us
    reshape x2, local copies, waits for them, and re-layouts, by_group(): array = array.reshape(tokens, group_count, -1, width)  3.5 us

profile of v1, /device:TPU:13, one launch (start us, length us, event | category | flops | bytes accessed | tf_op | source)
XLA Modules:
  0.0 148.4 jit_solution(2214165933039206111)
XLA Ops:
  0.6 0.0 copy-start
  0.6 0.6 pad_add_fusion.place
  1.3 0.1 and.21
  1.4 0.1 and.22
  1.5 0.7 select_reduce_fusion
  2.2 0.1 reduce_max.14
  2.3 0.1 reduce_max.18
  2.4 0.6 reshape.63.named
  3.0 0.9 copy.17
  3.9 0.7 reshape.64.lists
  4.6 2.1 %copy_bitcast_fusion = (bf16[8,192,128]{2,1,0:T(8,128)(2,1)}, bf16[8,192,128]{2,1,0:T(8,128)(2,1)}) fusion(bf16[192,8,128]{2,1,0:T(8,128)(2,1)} %param.7, bf16[192,8,128]{2,1,0:T(8,128)(2,1)} %param.6), kind=kLoop, calls=%fused_computation | loop fusion | bytes 1572864 | tf_op jit(solution)/shard_map/reshape | solution.py:284
  6.7 0.0 copy-done
  6.7 1.8 %copy.18 = bf16[192,8,4,128]{3,2,0,1:T(4,128)(2,1)} copy(bf16[192,8,4,128]{3,2,1,0:T(4,128)(2,1)S(1)} %bitcast.44) | data formatting | bytes 3145728 | tf_op jit(solution)/shard_map/reshape | solution.py:283
  8.5 0.0 copy-done.1
  8.5 1.8 %copy.19 = bf16[192,8,4,128]{3,2,0,1:T(4,128)(2,1)} copy(bf16[192,8,4,128]{3,2,1,0:T(4,128)(2,1)S(1)} %bitcast.45) | data formatting | bytes 3145728 | tf_op jit(solution)/shard_map/reshape | solution.py:283
  10.2 49.1 %bring.1 = (bf16[2,3072,128]{2,1,0:T(8,128)(2,1)}, bf16[2,3072,128]{2,1,0:T(8,128)(2,1)}, bf16[2,2,768,128]{3,2,1,0:T(8,128)(2,1)}, bf16[8,2,2,128,128]{4,3,2,1,0:T(8,128)(2,1)}) custom-call(s32[16]{0:T(128)} %reshape.63.named, bf16[8,768,128]{2,1,0:T(8,128)(2,1)} %bitcast.42, bf16[8,768,128]{2,1,0:T(8,128)(2,1)} %bitcast.43, ...), custom_call_target="tpu_custom_call" | custom-call | tf_op jit(solution)/shard_map/bring/pallas_call | solution.py:301
  59.3 34.8 %attend.1 = (bf16[2,3072,128]{2,1,0:T(8,128)(2,1)}, bf16[2,3072,128]{2,1,0:T(8,128)(2,1)}, bf16[2,2,768,128]{3,2,1,0:T(8,128)(2,1)}, bf16[8,2,2,128,128]{4,3,2,1,0:T(8,128)(2,1)}) custom-call(s32[2]{0:T(128)} %pad_add_fusion.place, s32[3072]{0:T(1024)} %reshape.64.lists, bf16[2,3072,128]{2,1,0:T(8,128)(2,1)} %get-tuple-element.15.q_ref, ...), custom_call_target="tpu_custom_call" | custom-call | tf_op jit(solution)/shard_map/attend/pallas_call | solution.py:321
  94.2 47.2 %give_back.1 = (bf16[8,768,128]{2,1,0:T(8,128)(2,1)}, bf16[8,768,128]{2,1,0:T(8,128)(2,1)}, bf16[2,8,192,128]{3,2,1,0:T(8,128)(2,1)}) custom-call(s32[16]{0:T(128)} %reshape.63.named, bf16[2,3072,128]{2,1,0:T(8,128)(2,1)} %get-tuple-element.19.outh_ref, bf16[2,3072,128]{2,1,0:T(8,128)(2,1)} %get-tuple-element.20.dqh_ref, ...), custom_call_target="tpu_custom_call" | custom-call | tf_op jit(solution)/shard_map/give_back/pallas_call | solution.py:355
  141.4 0.0 copy-start.2
  141.4 3.2 %copy.22 = bf16[192,8,4,128]{3,2,1,0:T(4,128)(2,1)} copy(bf16[192,8,4,128]{3,2,0,1:T(4,128)(2,1)} %bitcast.49) | data formatting | bytes 3145728 | tf_op jit(solution)/shard_map/transpose | solution.py:375
  144.6 1.7 %copy.23 = bf16[192,8,4,128]{3,2,1,0:T(4,128)(2,1)} copy(bf16[192,8,4,128]{3,2,0,1:T(4,128)(2,1)S(1)} %bitcast.48) | data formatting | bytes 3145728 | tf_op jit(solution)/shard_map/transpose | solution.py:375
  146.3 0.1 slice_bitcast_fusion
  146.4 1.0 copy.25
  147.4 1.0 copy.24
  (5 shorter events, 0.0 us)
Async XLA Ops:
  0.6 6.1 %copy-start = (bf16[192,32,128]{2,1,0:T(8,128)(2,1)S(1)}, bf16[192,32,128]{2,1,0:T(8,128)(2,1)}, u32[]{:S(2)}) copy-start(bf16[192,32,128]{2,1,0:T(8,128)(2,1)} %param.5) | copy-start | bytes 4718596
  6.7 1.8 %copy-start.1 = (bf16[192,32,128]{2,1,0:T(8,128)(2,1)S(1)}, bf16[192,32,128]{2,1,0:T(8,128)(2,1)}, u32[]{:S(2)}) copy-start(bf16[192,32,128]{2,1,0:T(8,128)(2,1)} %param.9) | copy-start | bytes 4718596
  141.4 3.2 %copy-start.2 = (bf16[8,768,128]{2,1,0:T(8,128)(2,1)S(1)}, bf16[8,768,128]{2,1,0:T(8,128)(2,1)}, u32[]{:S(2)}) copy-start(bf16[8,768,128]{2,1,0:T(8,128)(2,1)} %get-tuple-element.24) | copy-start | bytes 4718596
  144.6 1.7 %copy-start.3 = (bf16[2,8,192,128]{3,2,1,0:T(8,128)(2,1)S(1)}, bf16[2,8,192,128]{3,2,1,0:T(8,128)(2,1)}, u32[]{:S(2)}) copy-start(bf16[2,8,192,128]{3,2,1,0:T(8,128)(2,1)} %get-tuple-element.25) | copy-start | bytes 2359300

commit v2 on v1

--- a/solution.py
+++ b/solution.py
@@ -45,8 +45,8 @@
         return (
             (k_ref.at[part], kv_ref.at[0, :, pl.ds(pl.multiple_of(me * tokens, 64), tokens)]),
             (v_ref.at[part], kv_ref.at[1, :, pl.ds(pl.multiple_of(me * tokens, 64), tokens)]),
-            (q_ref.at[part], qh_ref.at[:, pl.ds(pl.multiple_of(me * rows, 128), rows)]),
-            (do_ref.at[part], doh_ref.at[:, pl.ds(pl.multiple_of(me * rows, 128), rows)]),
+            (q_ref.at[dest * groups], qh_ref.at[pl.ds(pl.multiple_of(me * rows, 128), rows)]),
+            (do_ref.at[dest * groups], doh_ref.at[pl.ds(pl.multiple_of(me * rows, 128), rows)]),
         )
 
     remote = {}
@@ -100,23 +100,22 @@
 
 
 def attend_kernel(
-    run_blocks, seq_blocks,
+    group, groups, run_blocks, seq_blocks,
     place, lists, q_ref, do_ref, kv_ref, recv_ref,
-    out_ref, dq_ref, own_ref, far_ref,
+    od_ref, own_ref, far_ref,
     k_buf, v_buf, acc_own, acc_far,
 ):
-    g, b = pl.program_id(0), pl.program_id(1)
-    groups = pl.num_programs(0)
+    g, b = 0, pl.program_id(0)
     base = place[1] * run_blocks
     scale = q_ref.shape[-1] ** -0.5
-    width = q_ref.shape[1] // BLOCK
+    width = q_ref.shape[0] // BLOCK
 
     @pl.when(b == 0)
     def _():
         acc_own[...] = jnp.zeros_like(acc_own)
         acc_far[...] = jnp.zeros_like(acc_far)
 
-    first = ((place[0] * groups + g) * seq_blocks + base + b) * TOPK
+    first = ((place[0] * groups + group) * seq_blocks + base + b) * TOPK
     slots = []
     for s in range(TOPK):
         listed = lists[first + s]
@@ -136,7 +135,7 @@
             k_buf[s * BLOCK : (s + 1) * BLOCK] = recv_ref[owner, 0, g]
             v_buf[s * BLOCK : (s + 1) * BLOCK] = recv_ref[owner, 1, g]
 
-    q, do = q_ref[0], do_ref[0]
+    q, do = q_ref[...], do_ref[...]
     keys, values = k_buf[...], v_buf[...]
     across = (((1,), (1,)), ((), ()))
     f32 = jnp.float32
@@ -157,7 +156,7 @@
     probs_b = probs.astype(jnp.bfloat16)
     out_t = lax.dot_general(values.T, probs_b, (((1,), (0,)), ((), ())), preferred_element_type=f32)
     out_b = out_t.T.astype(jnp.bfloat16)
-    out_ref[0] = out_b
+    od_ref[0] = out_b
     row_dot = jnp.sum(
         do.astype(f32).T * out_t.astype(jnp.bfloat16).astype(f32), axis=0, keepdims=True
     )
@@ -166,7 +165,7 @@
     dq_t = lax.dot_general(
         keys.T, grad_scores, (((1,), (0,)), ((), ())), preferred_element_type=f32
     )
-    dq_ref[0] = (dq_t * scale).T.astype(jnp.bfloat16)
+    od_ref[1] = (dq_t * scale).T.astype(jnp.bfloat16)
     dk = jnp.dot(grad_scores, q, preferred_element_type=f32)
     dv = jnp.dot(probs_b, do, preferred_element_type=f32)
     for s in range(TOPK):
@@ -186,42 +185,46 @@
 
     @pl.when(b == run_blocks - 1)
     def _():
-        own_ref[0, 0] = (acc_own[0] * scale).astype(jnp.bfloat16)
-        own_ref[1, 0] = acc_own[1].astype(jnp.bfloat16)
+        own_ref[0] = (acc_own[0] * scale).astype(jnp.bfloat16)
+        own_ref[1] = acc_own[1].astype(jnp.bfloat16)
         for j in range(acc_far.shape[0]):
-            far_ref[j, 0, 0] = (acc_far[j, 0] * scale).astype(jnp.bfloat16)
-            far_ref[j, 1, 0] = acc_far[j, 1].astype(jnp.bfloat16)
+            far_ref[j, 0] = (acc_far[j, 0] * scale).astype(jnp.bfloat16)
+            far_ref[j, 1] = acc_far[j, 1].astype(jnp.bfloat16)
 
 
 def return_kernel(
-    heads, peers, groups, run_blocks,
-    named, outh_ref, dqh_ref, own_ref, far_ref,
-    out_ref, dq_ref, kv_ref,
-    recv, stage, own_sem, head_send, head_recv, blk_send, blk_recv,
+    heads, peers, groups, run_blocks, named, *refs,
 ):
+    came, refs = refs[:heads], refs[heads:]
+    last_refs, refs = refs[: groups - 1], refs[groups - 1 :]
+    own_refs, refs = refs[:groups], refs[groups:]
+    far_refs, refs = refs[:groups], refs[groups:]
+    out_ref, dq_ref, kv_ref = refs[:3]
+    recv, stage, own_sem, came_sem, head_send, head_recv, blk_send, blk_recv = refs[3:]
     me, rank = greet(heads, peers)
     rows = out_ref.shape[1]
     tokens = kv_ref.shape[2]
     blk_copies = []
     for d in range(1, peers):
         peer = lax.rem(rank + d, peers)
-        copy = pltpu.make_async_remote_copy(
-            src_ref=far_ref.at[peer], dst_ref=recv.at[rank],
-            send_sem=blk_send.at[d], recv_sem=blk_recv.at[d],
-            device_id=(me, peer), device_id_type=MESH,
-        )
-        copy.start()
-        blk_copies.append(copy)
+        for g in range(groups):
+            copy = pltpu.make_async_remote_copy(
+                src_ref=far_refs[g].at[peer], dst_ref=recv.at[rank, g],
+                send_sem=blk_send.at[g, d], recv_sem=blk_recv.at[g, d],
+                device_id=(me, peer), device_id_type=MESH,
+            )
+            copy.start()
+            blk_copies.append(copy)
 
     def pieces(dest):
-        part = pl.ds(me * groups, groups)
         here = pl.ds(pl.multiple_of(dest * rows, 128), rows)
         some = pl.ds(pl.multiple_of(dest * tokens, 64), tokens)
-        return (
-            (outh_ref.at[:, here], out_ref.at[part]),
-            (dqh_ref.at[:, here], dq_ref.at[part]),
-            (stage.at[:, :, some], kv_ref.at[:, part]),
-        )
+        pairs = []
+        for g in range(1, groups):
+            pairs.append((last_refs[g - 1].at[0, here], out_ref.at[me * groups + g]))
+            pairs.append((last_refs[g - 1].at[1, here], dq_ref.at[me * groups + g]))
+        pairs.append((stage.at[:, :, some], kv_ref.at[:, pl.ds(me * groups, groups)]))
+        return pairs
 
     copies = []
 
@@ -241,8 +244,17 @@
         copy.start()
         copies.append(copy)
 
-    send(0)
-    send(1)
+    last = 2 * (groups - 1)
+    for n in range(last):
+        send(n)
+    for d in range(heads):
+        source = lax.rem(me + heads - d, heads)
+        for n, target in enumerate((out_ref, dq_ref)):
+            copy = pltpu.make_async_copy(
+                came[d].at[n], target.at[source * groups], came_sem.at[n, d]
+            )
+            copy.start()
+            copies.append(copy)
     for copy in blk_copies:
         copy.wait()
     for g in range(groups):
@@ -253,15 +265,15 @@
                 def add(d, total):
                     peer = lax.rem(rank + d, peers)
                     weight = (named[g * peers + peer] == i).astype(jnp.float32)
-                    return total + weight * recv[peer, n, g].astype(jnp.float32)
-
-                total = own_ref[n, g, at, :].astype(jnp.float32)
+                    return total + weight * recv[peer, g, n].astype(jnp.float32)
+
+                total = own_refs[g][n, at, :].astype(jnp.float32)
                 total = lax.fori_loop(1, peers, add, total)
                 stage[n, g, at, :] = total.astype(jnp.bfloat16)
                 return 0
 
             lax.fori_loop(0, run_blocks, settle, 0)
-    send(2)
+    send(last)
     for copy in copies:
         copy.wait()
 
@@ -297,7 +309,8 @@
     )
     far_shape = (peers, 2, groups, BLOCK, width)
     own_shape = (2, groups, run_len, width)
-    q_shape = (groups, rows * heads, width)
+    q_shape = (rows * heads, width)
+    q_t, do_t = by_group(queries), by_group(grad_out)
     qh, doh, kv, recv = pl.pallas_call(
         functools.partial(bring_kernel, heads, peers, groups, run_blocks),
         out_shape=(
@@ -314,43 +327,83 @@
         ],
         compiler_params=params(collective_id=0),
         name="bring",
-    )(named, by_group(queries), by_group(grad_out), by_group(rotated_keys), by_group(value_vectors))
+    )(named, q_t, do_t, by_group(rotated_keys), by_group(value_vectors))
 
     place = jnp.stack([me, rank]).astype(jnp.int32)
-    item = pl.BlockSpec((1, BLOCK * per_group, width), lambda g, b, *_: (g, b, 0))
-    outh, dqh, own, far = pl.pallas_call(
-        functools.partial(attend_kernel, run_blocks, seq_blocks),
-        grid_spec=pltpu.PrefetchScalarGridSpec(
-            num_scalar_prefetch=2,
-            grid=(groups, run_blocks),
-            in_specs=[
-                item, item,
-                pl.BlockSpec(own_shape, lambda g, b, *_: (0, 0, 0, 0)),
-                pl.BlockSpec(far_shape, lambda g, b, *_: (0, 0, 0, 0, 0)),
-            ],
-            out_specs=(
-                item, item,
-                pl.BlockSpec((2, 1, run_len, width), lambda g, b, *_: (0, g, 0, 0)),
-                pl.BlockSpec((peers, 2, 1, BLOCK, width), lambda g, b, *_: (0, 0, g, 0, 0)),
+    flat_lists = block_list.reshape(-1)
+    ring = [[(i, (i + d) % heads) for i in range(heads)] for d in range(heads)]
+
+    def both(at):
+        return jnp.stack(
+            [lax.dynamic_index_in_dim(array, at, 0, keepdims=False) for array in (q_t, do_t)]
+        )
+
+    def fetch(group, after):
+        whole = jnp.zeros((2, rows * heads, width), bf16)
+        for d in range(heads):
+            piece = both(lax.rem(me + d, heads) * groups + group)
+            if d:
+                piece, _ = lax.optimization_barrier((piece, after))
+                piece = lax.ppermute(piece, "head", ring[d])
+            source = lax.rem(me + heads - d, heads)
+            whole = lax.dynamic_update_slice(whole, piece, (0, source * rows, 0))
+        return whole
+
+    item_rows = BLOCK * per_group
+    item = pl.BlockSpec((item_rows, width), lambda b, *_: (b, 0))
+
+    def attend(group, q_spec, do_spec, q, do):
+        return pl.pallas_call(
+            functools.partial(attend_kernel, group, groups, run_blocks, seq_blocks),
+            grid_spec=pltpu.PrefetchScalarGridSpec(
+                num_scalar_prefetch=2,
+                grid=(run_blocks,),
+                in_specs=[
+                    q_spec, do_spec,
+                    pl.BlockSpec((2, 1, run_len, width), lambda b, *_: (0, group, 0, 0)),
+                    pl.BlockSpec((peers, 2, 1, BLOCK, width), lambda b, *_: (0, 0, group, 0, 0)),
+                ],
+                out_specs=(
+                    pl.BlockSpec((2, item_rows, width), lambda b, *_: (0, b, 0)),
+                    pl.BlockSpec((2, run_len, width), lambda b, *_: (0, 0, 0)),
+                    pl.BlockSpec((peers, 2, BLOCK, width), lambda b, *_: (0, 0, 0, 0)),
+                ),
+                scratch_shapes=[
+                    pltpu.VMEM((TOPK * BLOCK, width), bf16),
+                    pltpu.VMEM((TOPK * BLOCK, width), bf16),
+                    pltpu.VMEM((2, run_len, width), jnp.float32),
+                    pltpu.VMEM((peers, 2, BLOCK, width), jnp.float32),
+                ],
             ),
-            scratch_shapes=[
-                pltpu.VMEM((TOPK * BLOCK, width), bf16),
-                pltpu.VMEM((TOPK * BLOCK, width), bf16),
-                pltpu.VMEM((2, run_len, width), jnp.float32),
-                pltpu.VMEM((peers, 2, BLOCK, width), jnp.float32),
-            ],
-        ),
-        out_shape=(
-            jax.ShapeDtypeStruct(q_shape, bf16),
-            jax.ShapeDtypeStruct(q_shape, bf16),
-            jax.ShapeDtypeStruct(own_shape, bf16),
-            jax.ShapeDtypeStruct(far_shape, bf16),
-        ),
-        compiler_params=pltpu.CompilerParams(
-            dimension_semantics=("arbitrary", "arbitrary"), vmem_limit_bytes=VMEM_LIMIT
-        ),
-        name="attend",
-    )(place, block_list.reshape(-1), qh, doh, kv, recv)
+            out_shape=(
+                jax.ShapeDtypeStruct((2, rows * heads, width), bf16),
+                jax.ShapeDtypeStruct((2, run_len, width), bf16),
+                jax.ShapeDtypeStruct((peers, 2, BLOCK, width), bf16),
+            ),
+            compiler_params=pltpu.CompilerParams(
+                dimension_semantics=("arbitrary",), vmem_limit_bytes=VMEM_LIMIT
+            ),
+            cost_estimate=pl.CostEstimate(
+                flops=run_blocks * 12 * item_rows * TOPK * BLOCK * width,
+                bytes_accessed=8 * rows * heads * width,
+                transcendentals=run_blocks * item_rows * TOPK * BLOCK,
+            ),
+            name=f"attend_{group}",
+        )(place, flat_lists, q, do, kv, recv)
+
+    results = [attend(0, item, item, qh, doh)]
+    both_specs = [
+        pl.BlockSpec((None, item_rows, width), lambda b, *_, n=n: (n, b, 0)) for n in range(2)
+    ]
+    for group in range(1, groups):
+        moved = fetch(group, qh)
+        results.append(attend(group, *both_specs, moved, moved))
+    first_out = results[0][0]
+    came = []
+    for d in range(heads):
+        start = lax.rem(me + d, heads) * rows
+        piece = lax.dynamic_slice_in_dim(first_out, start, rows, 1)
+        came.append(lax.ppermute(piece, "head", ring[d]) if d else piece)
 
     out_g, dq_g, kv_g = pl.pallas_call(
         functools.partial(return_kernel, heads, peers, groups, run_blocks),
@@ -359,16 +412,27 @@
             jax.ShapeDtypeStruct((group_count, rows, width), bf16),
             jax.ShapeDtypeStruct((2, group_count, tokens, width), bf16),
         ),
-        in_specs=[smem, any_space, any_space, vmem, any_space],
+        in_specs=[smem]
+        + [any_space] * (heads + groups - 1)
+        + [vmem] * groups
+        + [any_space] * groups,
         out_specs=(any_space, any_space, any_space),
         scratch_shapes=[
-            pltpu.VMEM(far_shape, bf16),
+            pltpu.VMEM((peers, groups, 2, BLOCK, width), bf16),
             pltpu.VMEM(own_shape, bf16),
-            dma((3,)), dma((3, heads)), dma((3, heads)), dma((peers,)), dma((peers,)),
+            dma((2 * groups - 1,)), dma((2, heads)),
+            dma((2 * groups - 1, heads)), dma((2 * groups - 1, heads)),
+            dma((groups, peers)), dma((groups, peers)),
         ],
         compiler_params=params(collective_id=1),
         name="give_back",
-    )(named, outh, dqh, own, far)
+    )(
+        named,
+        *came,
+        *[result[0] for result in results[1:]],
+        *[result[1] for result in results],
+        *[result[2] for result in results],
+    )
 
     def by_token(array, count):
         array = array.reshape(group_count, tokens, count, width)

time: 151 us -> 171 us (1.13)
  the two profiles are of different devices: /device:TPU:13 before, /device:TPU:0 now
where the time goes in v2:
time: 171 us
  Pallas kernels  143 us (84%)
  local copies, waits for them, and re-layouts  19.1 us (11%)
  starting transfers between devices  5.52 us (3%)
  other arithmetic  1.74 us (1%)
    pallas_call x1, Pallas kernels, on_device(): pl.pallas_call(functools.partial(return_kernel, heads, peers, groups, run...  72.2 us
    pallas_call x2, Pallas kernels, attend(): pl.pallas_call(functools.partial(attend_kernel, group, groups, run_blocks...  37 us
    pallas_call x1, Pallas kernels, on_device(): pl.pallas_call(functools.partial(bring_kernel, heads, peers, groups, run_...  34.3 us
    unnamed x29, local copies, waits for them, and re-layouts  5.9 us
    transpose x2, local copies, waits for them, and re-layouts, by_token(): jnp.transpose(array, (1, 0, 2, 3))  4.89 us
  transfers between devices with their start and end apart: 6, of which 0 were waited for; matrix products, arithmetic and copies ran while one was open for 3% of the time, Pallas kernels for 22%

profile of v2, /device:TPU:0, one launch (start us, length us, event | category | flops | bytes accessed | tf_op | source)
XLA Modules:
  0.0 170.8 jit_solution(7274677438864383510)
XLA Ops:
  0.7 2.1 %copy.18 = bf16[192,8,4,128]{3,2,0,1:T(4,128)(2,1)S(1)} copy(bf16[192,8,4,128]{3,2,1,0:T(4,128)(2,1)} %bitcast.46) | data formatting | bytes 3145728 | tf_op jit(solution)/shard_map/reshape | solution.py:295
  3.5 0.8 select_reduce_fusion
  4.5 0.7 reshape.63.named
  5.4 0.8 copy-done.9
  6.3 1.0 copy_bitcast_fusion
  7.3 34.3 %bring.1 = (bf16[3072,128]{1,0:T(8,128)(2,1)}, bf16[3072,128]{1,0:T(8,128)(2,1)}, bf16[2,2,768,128]{3,2,1,0:T(8,128)(2,1)}, bf16[8,2,2,128,128]{4,3,2,1,0:T(8,128)(2,1)}) custom-call(s32[16]{0:T(128)} %reshape.63.named, bf16[8,768,128]{2,1,0:T(8,128)(2,1)} %bitcast.43, bf16[8,768,128]{2,1,0:T(8,128)(2,1)} %bitcast.45, ...), custom_call_target="tpu_custom_call" | custom-call | tf_op jit(solution)/shard_map/bring/pallas_call | solution.py:314
  41.6 1.9 %collective-permute-start.3 = (bf16[2,768,128]{2,1,0:T(8,128)(2,1)S(1)}, bf16[2,768,128]{2,1,0:T(8,128)(2,1)S(1)}, u32[]{:S(2)}, u32[]{:S(2)}) collective-permute-start(bf16[2,768,128]{2,1,0:T(8,128)(2,1)S(1)} %pad_maximum_fusion), channel_id=1, source_target_pairs={{0,8},{8,16},{16,24},{24,0},{1,9},{9,17},{17,25},{25,1},{2,10},{10... | collective-permute-start | bytes 1179656 | tf_op jit(solution)/shard_map/ppermute | solution.py:347
  43.5 0.6 collective-permute-start.4
  44.1 0.9 collective-permute-start.5
  45.1 0.7 reshape.64.lists
  45.9 0.7 pad_add_fusion.place
  46.5 18.5 %attend_0.1 = (bf16[2,3072,128]{2,1,0:T(8,128)(2,1)}, bf16[2,768,128]{2,1,0:T(8,128)(2,1)}, bf16[8,2,128,128]{3,2,1,0:T(8,128)(2,1)}) custom-call(s32[2]{0:T(128)} %pad_add_fusion.place, s32[3072]{0:T(1024)} %reshape.64.lists, bf16[3072,128]{1,0:T(8,128)(2,1)} %get-tuple-element.20.q_ref, bf16[3072,128]{1,0:T(8,128)(2,1)} %get-tuple-element.21.do_ref, ...), custom_call_target="tpu_custom_call" | custom-call | flops 4831838208 | bytes 3145728 | tf_op jit(solution)/shard_map/attend_0/pallas_call | solution.py:356
  65.1 2.5 %constant_dynamic-slice_fusion.8 = (bf16[2,768,128]{2,1,0:T(8,128)(2,1)}, bf16[2,768,128]{2,1,0:T(8,128)(2,1)}, bf16[2,768,128]{2,1,0:T(8,128)(2,1)}, bf16[2,768,128]{2,1,0:T(8,128)(2,1)}) fusion(bf16[2,3072,128]{2,1,0:T(8,128)(2,1)} %get-tuple-element.24, s32[]{:T(128)S(6)} %select_n.55, s32[]{:T(128)S(6)} %select_n.54, s32[]{:T(128)S(6)} %select_n.53, ...), kind=kLoop, calls=%fused_computation.25 | loop fusion | bytes 3145744 | tf_op jit(solution)/shard_map/dynamic_slice | solution.py:405
  67.6 1.2 collective-permute-start.1
  69.1 0.7 copy-done.11
  69.8 1.0 collective-permute-start.2
  71.0 1.1 copy-done.4
  72.1 18.5 %attend_1.1 = (bf16[2,3072,128]{2,1,0:T(8,128)(2,1)}, bf16[2,768,128]{2,1,0:T(8,128)(2,1)}, bf16[8,2,128,128]{3,2,1,0:T(8,128)(2,1)}) custom-call(s32[2]{0:T(128)} %pad_add_fusion.place, s32[3072]{0:T(1024)} %reshape.64.lists, bf16[2,3072,128]{2,1,0:T(8,128)(2,1)} %copy-done.4, bf16[2,3072,128]{2,1,0:T(8,128)(2,1)} %copy-done.4, ...), custom_call_target="tpu_custom_call" | custom-call | flops 4831838208 | bytes 3145728 | tf_op jit(solution)/shard_map/attend_1/pallas_call | solution.py:356
  90.7 0.7 copy-done.6
  91.6 72.2 %give_back.1 = (bf16[8,768,128]{2,1,0:T(8,128)(2,1)}, bf16[8,768,128]{2,1,0:T(8,128)(2,1)}, bf16[2,8,192,128]{3,2,1,0:T(8,128)(2,1)}) custom-call(s32[16]{0:T(128)} %reshape.63.named, bf16[2,768,128]{2,1,0:T(8,128)(2,1)} %get-tuple-element.55.refs_0_, bf16[2,768,128]{2,1,0:T(8,128)(2,1)} %copy-done.6, bf16[2,768,128]{2,1,0:T(8,128)(2,1)} %copy-done.7, ...), custom_call_target="tpu_custom_call" | custom-call | tf_op jit(solution)/shard_map/give_back/pallas_call | solution.py:408
  163.8 3.2 %copy.22 = bf16[192,8,4,128]{3,2,1,0:T(4,128)(2,1)} copy(bf16[192,8,4,128]{3,2,0,1:T(4,128)(2,1)} %bitcast.51) | data formatting | bytes 3145728 | tf_op jit(solution)/shard_map/transpose | solution.py:439
  167.1 1.7 copy.23
  168.8 1.0 copy.24
  169.8 1.0 copy.25
  (46 shorter events, 2.2 us)
Async XLA Ops:
  0.7 2.1 %copy-start.2 = (bf16[192,32,128]{2,1,0:T(8,128)(2,1)S(1)}, bf16[192,32,128]{2,1,0:T(8,128)(2,1)}, u32[]{:S(2)}) copy-start(bf16[192,32,128]{2,1,0:T(8,128)(2,1)} %param.9) | copy-start | bytes 4718596
  2.8 2.4 %copy-start = (bf16[192,8,4,128]{3,2,0,1:T(4,128)(2,1)}, bf16[192,8,4,128]{3,2,0,1:T(4,128)(2,1)S(1)}, u32[]{:S(2)}) copy-start(bf16[192,8,4,128]{3,2,0,1:T(4,128)(2,1)S(1)} %copy.18) | copy-start | bytes 4718596
  3.3 2.0 %copy-start.1 = (bf16[192,8,4,128]{3,2,0,1:T(4,128)(2,1)}, bf16[192,8,4,128]{3,2,0,1:T(4,128)(2,1)S(1)}, u32[]{:S(2)}) copy-start(bf16[192,8,4,128]{3,2,0,1:T(4,128)(2,1)S(1)} %copy.19) | copy-start | bytes 4718596
  5.2 1.0 copy-start.9
  5.2 1.1 copy-start.10
  41.6 3.5 %copy-start.12 = (s32[8,48,8]{1,2,0:T(8,128)S(1)}, s32[8,48,8]{1,2,0:T(8,128)}, u32[]{:S(2)}) copy-start(s32[8,48,8]{1,2,0:T(8,128)} %param.8) | copy-start | bytes 36868
  41.6 27.5 %collective-permute-start.3 = (bf16[2,768,128]{2,1,0:T(8,128)(2,1)S(1)}, bf16[2,768,128]{2,1,0:T(8,128)(2,1)S(1)}, u32[]{:S(2)}, u32[]{:S(2)}) collective-permute-start(bf16[2,768,128]{2,1,0:T(8,128)(2,1)S(1)} %pad_maximum_fusion), channel_id=1, source_target_pairs={{0,8},{8,16},{16,24},{24,0},{1,9},{9,17},{17,25},{25,1},{2,10},{10... | collective-permute-start | bytes 1179656 | tf_op jit(solution)/shard_map/ppermute | solution.py:347
  43.5 27.3 %collective-permute-start.4 = (bf16[2,768,128]{2,1,0:T(8,128)(2,1)S(1)}, bf16[2,768,128]{2,1,0:T(8,128)(2,1)S(1)}, u32[]{:S(2)}, u32[]{:S(2)}) collective-permute-start(bf16[2,768,128]{2,1,0:T(8,128)(2,1)S(1)} %pad_maximum_fusion.1), channel_id=1, source_target_pairs={{0,16},{8,24},{16,0},{24,8},{1,17},{9,25},{17,1},{25,9},{2,18},{10... | collective-permute-start | bytes 1179656 | tf_op jit(solution)/shard_map/ppermute | solution.py:347
  44.1 26.7 %collective-permute-start.5 = (bf16[2,768,128]{2,1,0:T(8,128)(2,1)S(1)}, bf16[2,768,128]{2,1,0:T(8,128)(2,1)S(1)}, u32[]{:S(2)}, u32[]{:S(2)}) collective-permute-start(bf16[2,768,128]{2,1,0:T(8,128)(2,1)S(1)} %pad_maximum_fusion.2), channel_id=1, source_target_pairs={{0,24},{8,0},{16,8},{24,16},{1,25},{9,1},{17,9},{25,17},{2,26},{10... | collective-permute-start | bytes 1179656 | tf_op jit(solution)/shard_map/ppermute | solution.py:347
  67.6 23.0 %collective-permute-start = (bf16[2,768,128]{2,1,0:T(8,128)(2,1)}, bf16[2,768,128]{2,1,0:T(8,128)(2,1)S(1)}, u32[]{:S(2)}, u32[]{:S(2)}) collective-permute-start(bf16[2,768,128]{2,1,0:T(8,128)(2,1)} %get-tuple-element.54), channel_id=1, source_target_pairs={{0,8},{8,16},{16,24},{24,0},{1,9},{9,17},{17,25},{25,1},{2,10},{10... | collective-permute-start | bytes 1179656 | tf_op jit(solution)/shard_map/ppermute | solution.py:406
  67.6 23.0 %collective-permute-start.1 = (bf16[2,768,128]{2,1,0:T(8,128)(2,1)}, bf16[2,768,128]{2,1,0:T(8,128)(2,1)S(1)}, u32[]{:S(2)}, u32[]{:S(2)}) collective-permute-start(bf16[2,768,128]{2,1,0:T(8,128)(2,1)} %get-tuple-element.53), channel_id=1, source_target_pairs={{0,16},{8,24},{16,0},{24,8},{1,17},{9,25},{17,1},{25,9},{2,18},{10... | collective-permute-start | bytes 1179656 | tf_op jit(solution)/shard_map/ppermute | solution.py:406
  68.8 1.0 copy-start.11
  69.8 20.9 %collective-permute-start.2 = (bf16[2,768,128]{2,1,0:T(8,128)(2,1)S(1)}, bf16[2,768,128]{2,1,0:T(8,128)(2,1)S(1)}, u32[]{:S(2)}, u32[]{:S(2)}) collective-permute-start(bf16[2,768,128]{2,1,0:T(8,128)(2,1)S(1)} %copy-done.11), channel_id=1, source_target_pairs={{0,24},{8,0},{16,8},{24,16},{1,25},{9,1},{17,9},{25,17},{2,26},{10... | collective-permute-start | bytes 1179656 | tf_op jit(solution)/shard_map/ppermute | solution.py:406
  71.0 1.1 copy-start.4
  90.6 0.7 copy-start.6
  90.6 0.9 copy-start.7
  90.7 1.0 copy-start.8
  163.8 3.2 %copy-start.3 = (bf16[8,768,128]{2,1,0:T(8,128)(2,1)S(1)}, bf16[8,768,128]{2,1,0:T(8,128)(2,1)}, u32[]{:S(2)}) copy-start(bf16[8,768,128]{2,1,0:T(8,128)(2,1)} %get-tuple-element.34) | copy-start | bytes 4718596
  167.0 1.7 copy-start.5

commit v3 on v2

--- a/solution.py
+++ b/solution.py
@@ -413,7 +413,8 @@
             jax.ShapeDtypeStruct((2, group_count, tokens, width), bf16),
         ),
         in_specs=[smem]
-        + [any_space] * (heads + groups - 1)
+        + [vmem] * heads
+        + [any_space] * (groups - 1)
         + [vmem] * groups
         + [any_space] * groups,
         out_specs=(any_space, any_space, any_space),

time: 171 us -> 145 us (0.85)
  the two profiles are of different devices: /device:TPU:0 before, /device:TPU:13 now
where the time goes in v3:
time: 145 us
  Pallas kernels  119 us (82%)
  local copies, waits for them, and re-layouts  19.1 us (13%)
  starting transfers between devices  4.06 us (3%)
  other arithmetic  1.74 us (1%)
    pallas_call x1, Pallas kernels, on_device(): pl.pallas_call(functools.partial(return_kernel, heads, peers, groups, run...  41.5 us
    pallas_call x1, Pallas kernels, on_device(): pl.pallas_call(functools.partial(bring_kernel, heads, peers, groups, run_...  40.4 us
    pallas_call x2, Pallas kernels, attend(): pl.pallas_call(functools.partial(attend_kernel, group, groups, run_blocks...  37.1 us
    unnamed x29, local copies, waits for them, and re-layouts  5.9 us
    transpose x2, local copies, waits for them, and re-layouts, by_token(): jnp.transpose(array, (1, 0, 2, 3))  4.89 us
  transfers between devices with their start and end apart: 6, of which 0 were waited for; matrix products, arithmetic and copies ran while one was open for 3% of the time, Pallas kernels for 26%

profile of v3, /device:TPU:13, one launch (start us, length us, event | category | flops | bytes accessed | tf_op | source)
XLA Modules:
  0.0 144.9 jit_solution(7280688391796390515)
XLA Ops:
  0.7 2.1 %copy.18 = bf16[192,8,4,128]{3,2,0,1:T(4,128)(2,1)S(1)} copy(bf16[192,8,4,128]{3,2,1,0:T(4,128)(2,1)} %bitcast.46) | data formatting | bytes 3145728 | tf_op jit(solution)/shard_map/reshape | solution.py:295
  2.8 0.5 copy.19
  3.5 0.8 select_reduce_fusion
  4.5 0.7 reshape.63.named
  5.4 0.8 copy-done.9
  6.3 1.0 copy_bitcast_fusion
  7.3 40.4 %bring.1 = (bf16[3072,128]{1,0:T(8,128)(2,1)}, bf16[3072,128]{1,0:T(8,128)(2,1)}, bf16[2,2,768,128]{3,2,1,0:T(8,128)(2,1)}, bf16[8,2,2,128,128]{4,3,2,1,0:T(8,128)(2,1)}) custom-call(s32[16]{0:T(128)} %reshape.63.named, bf16[8,768,128]{2,1,0:T(8,128)(2,1)} %bitcast.43, bf16[8,768,128]{2,1,0:T(8,128)(2,1)} %bitcast.45, ...), custom_call_target="tpu_custom_call" | custom-call | tf_op jit(solution)/shard_map/bring/pallas_call | solution.py:314
  47.8 0.5 collective-permute-start.3
  48.3 1.3 collective-permute-start.4
  49.9 0.7 reshape.64.lists
  50.6 0.7 pad_add_fusion.place
  51.3 18.5 %attend_0.1 = (bf16[2,3072,128]{2,1,0:T(8,128)(2,1)}, bf16[2,768,128]{2,1,0:T(8,128)(2,1)}, bf16[8,2,128,128]{3,2,1,0:T(8,128)(2,1)}) custom-call(s32[2]{0:T(128)} %pad_add_fusion.place, s32[3072]{0:T(1024)} %reshape.64.lists, bf16[3072,128]{1,0:T(8,128)(2,1)} %get-tuple-element.20.q_ref, bf16[3072,128]{1,0:T(8,128)(2,1)} %get-tuple-element.21.do_ref, ...), custom_call_target="tpu_custom_call" | custom-call | flops 4831838208 | bytes 3145728 | tf_op jit(solution)/shard_map/attend_0/pallas_call | solution.py:356
  69.8 2.5 %constant_dynamic-slice_fusion.8 = (bf16[2,768,128]{2,1,0:T(8,128)(2,1)}, bf16[2,768,128]{2,1,0:T(8,128)(2,1)}, bf16[2,768,128]{2,1,0:T(8,128)(2,1)}, bf16[2,768,128]{2,1,0:T(8,128)(2,1)}) fusion(bf16[2,3072,128]{2,1,0:T(8,128)(2,1)} %get-tuple-element.24, s32[]{:T(128)S(6)} %select_n.55, s32[]{:T(128)S(6)} %select_n.54, s32[]{:T(128)S(6)} %select_n.53, ...), kind=kLoop, calls=%fused_computation.25 | loop fusion | bytes 3145744 | tf_op jit(solution)/shard_map/dynamic_slice | solution.py:405
  72.4 1.7 %collective-permute-start = (bf16[2,768,128]{2,1,0:T(8,128)(2,1)}, bf16[2,768,128]{2,1,0:T(8,128)(2,1)S(1)}, u32[]{:S(2)}, u32[]{:S(2)}) collective-permute-start(bf16[2,768,128]{2,1,0:T(8,128)(2,1)} %get-tuple-element.54), channel_id=1, source_target_pairs={{0,8},{8,16},{16,24},{24,0},{1,9},{9,17},{17,25},{25,1},{2,10},{10... | collective-permute-start | bytes 1179656 | tf_op jit(solution)/shard_map/ppermute | solution.py:406
  74.5 0.7 copy-done.11
  75.3 0.2 collective-permute-start.2
  75.7 1.1 copy-done.4
  76.8 18.5 %attend_1.1 = (bf16[2,3072,128]{2,1,0:T(8,128)(2,1)}, bf16[2,768,128]{2,1,0:T(8,128)(2,1)}, bf16[8,2,128,128]{3,2,1,0:T(8,128)(2,1)}) custom-call(s32[2]{0:T(128)} %pad_add_fusion.place, s32[3072]{0:T(1024)} %reshape.64.lists, bf16[2,3072,128]{2,1,0:T(8,128)(2,1)} %copy-done.4, bf16[2,3072,128]{2,1,0:T(8,128)(2,1)} %copy-done.4, ...), custom_call_target="tpu_custom_call" | custom-call | flops 4831838208 | bytes 3145728 | tf_op jit(solution)/shard_map/attend_1/pallas_call | solution.py:356
  95.5 0.7 copy-done.6
  96.4 41.5 %give_back.1 = (bf16[8,768,128]{2,1,0:T(8,128)(2,1)}, bf16[8,768,128]{2,1,0:T(8,128)(2,1)}, bf16[2,8,192,128]{3,2,1,0:T(8,128)(2,1)}) custom-call(s32[16]{0:T(128)} %reshape.63.named, bf16[2,768,128]{2,1,0:T(8,128)(2,1)} %get-tuple-element.55.refs_0_, bf16[2,768,128]{2,1,0:T(8,128)(2,1)} %copy-done.6, bf16[2,768,128]{2,1,0:T(8,128)(2,1)} %copy-done.7, ...), custom_call_target="tpu_custom_call" | custom-call | tf_op jit(solution)/shard_map/give_back/pallas_call | solution.py:408
  137.9 3.2 %copy.22 = bf16[192,8,4,128]{3,2,1,0:T(4,128)(2,1)} copy(bf16[192,8,4,128]{3,2,0,1:T(4,128)(2,1)} %bitcast.51) | data formatting | bytes 3145728 | tf_op jit(solution)/shard_map/transpose | solution.py:440
  141.1 1.7 %copy.23 = bf16[192,8,4,128]{3,2,1,0:T(4,128)(2,1)} copy(bf16[192,8,4,128]{3,2,0,1:T(4,128)(2,1)S(1)} %bitcast.50) | data formatting | bytes 3145728 | tf_op jit(solution)/shard_map/transpose | solution.py:440
  142.8 1.0 copy.24
  143.8 1.0 copy.25
  (46 shorter events, 1.9 us)
Async XLA Ops:
  0.7 2.1 %copy-start.2 = (bf16[192,32,128]{2,1,0:T(8,128)(2,1)S(1)}, bf16[192,32,128]{2,1,0:T(8,128)(2,1)}, u32[]{:S(2)}) copy-start(bf16[192,32,128]{2,1,0:T(8,128)(2,1)} %param.9) | copy-start | bytes 4718596
  2.8 2.4 %copy-start = (bf16[192,8,4,128]{3,2,0,1:T(4,128)(2,1)}, bf16[192,8,4,128]{3,2,0,1:T(4,128)(2,1)S(1)}, u32[]{:S(2)}) copy-start(bf16[192,8,4,128]{3,2,0,1:T(4,128)(2,1)S(1)} %copy.18) | copy-start | bytes 4718596
  3.3 2.0 %copy-start.1 = (bf16[192,8,4,128]{3,2,0,1:T(4,128)(2,1)}, bf16[192,8,4,128]{3,2,0,1:T(4,128)(2,1)S(1)}, u32[]{:S(2)}) copy-start(bf16[192,8,4,128]{3,2,0,1:T(4,128)(2,1)S(1)} %copy.19) | copy-start | bytes 4718596
  5.2 1.0 copy-start.9
  5.2 1.1 copy-start.10
  47.7 2.0 %copy-start.12 = (s32[8,48,8]{1,2,0:T(8,128)S(1)}, s32[8,48,8]{1,2,0:T(8,128)}, u32[]{:S(2)}) copy-start(s32[8,48,8]{1,2,0:T(8,128)} %param.8) | copy-start | bytes 36868
  47.8 26.8 %collective-permute-start.3 = (bf16[2,768,128]{2,1,0:T(8,128)(2,1)S(1)}, bf16[2,768,128]{2,1,0:T(8,128)(2,1)S(1)}, u32[]{:S(2)}, u32[]{:S(2)}) collective-permute-start(bf16[2,768,128]{2,1,0:T(8,128)(2,1)S(1)} %pad_maximum_fusion), channel_id=1, source_target_pairs={{0,8},{8,16},{16,24},{24,0},{1,9},{9,17},{17,25},{25,1},{2,10},{10... | collective-permute-start | bytes 1179656 | tf_op jit(solution)/shard_map/ppermute | solution.py:347
  48.3 27.2 %collective-permute-start.4 = (bf16[2,768,128]{2,1,0:T(8,128)(2,1)S(1)}, bf16[2,768,128]{2,1,0:T(8,128)(2,1)S(1)}, u32[]{:S(2)}, u32[]{:S(2)}) collective-permute-start(bf16[2,768,128]{2,1,0:T(8,128)(2,1)S(1)} %pad_maximum_fusion.1), channel_id=1, source_target_pairs={{0,16},{8,24},{16,0},{24,8},{1,17},{9,25},{17,1},{25,9},{2,18},{10... | collective-permute-start | bytes 1179656 | tf_op jit(solution)/shard_map/ppermute | solution.py:347
  49.7 25.9 %collective-permute-start.5 = (bf16[2,768,128]{2,1,0:T(8,128)(2,1)S(1)}, bf16[2,768,128]{2,1,0:T(8,128)(2,1)S(1)}, u32[]{:S(2)}, u32[]{:S(2)}) collective-permute-start(bf16[2,768,128]{2,1,0:T(8,128)(2,1)S(1)} %pad_maximum_fusion.2), channel_id=1, source_target_pairs={{0,24},{8,0},{16,8},{24,16},{1,25},{9,1},{17,9},{25,17},{2,26},{10... | collective-permute-start | bytes 1179656 | tf_op jit(solution)/shard_map/ppermute | solution.py:347
  72.4 23.0 %collective-permute-start = (bf16[2,768,128]{2,1,0:T(8,128)(2,1)}, bf16[2,768,128]{2,1,0:T(8,128)(2,1)S(1)}, u32[]{:S(2)}, u32[]{:S(2)}) collective-permute-start(bf16[2,768,128]{2,1,0:T(8,128)(2,1)} %get-tuple-element.54), channel_id=1, source_target_pairs={{0,8},{8,16},{16,24},{24,0},{1,9},{9,17},{17,25},{25,1},{2,10},{10... | collective-permute-start | bytes 1179656 | tf_op jit(solution)/shard_map/ppermute | solution.py:406
  74.1 21.3 %collective-permute-start.1 = (bf16[2,768,128]{2,1,0:T(8,128)(2,1)}, bf16[2,768,128]{2,1,0:T(8,128)(2,1)S(1)}, u32[]{:S(2)}, u32[]{:S(2)}) collective-permute-start(bf16[2,768,128]{2,1,0:T(8,128)(2,1)} %get-tuple-element.53), channel_id=1, source_target_pairs={{0,16},{8,24},{16,0},{24,8},{1,17},{9,25},{17,1},{25,9},{2,18},{10... | collective-permute-start | bytes 1179656 | tf_op jit(solution)/shard_map/ppermute | solution.py:406
  74.3 1.0 copy-start.11
  75.3 20.2 %collective-permute-start.2 = (bf16[2,768,128]{2,1,0:T(8,128)(2,1)S(1)}, bf16[2,768,128]{2,1,0:T(8,128)(2,1)S(1)}, u32[]{:S(2)}, u32[]{:S(2)}) collective-permute-start(bf16[2,768,128]{2,1,0:T(8,128)(2,1)S(1)} %copy-done.11), channel_id=1, source_target_pairs={{0,24},{8,0},{16,8},{24,16},{1,25},{9,1},{17,9},{25,17},{2,26},{10... | collective-permute-start | bytes 1179656 | tf_op jit(solution)/shard_map/ppermute | solution.py:406
  75.7 1.1 copy-start.4
  95.4 0.7 copy-start.6
  95.4 0.9 copy-start.7
  95.4 1.0 copy-start.8
  137.9 3.2 %copy-start.3 = (bf16[8,768,128]{2,1,0:T(8,128)(2,1)S(1)}, bf16[8,768,128]{2,1,0:T(8,128)(2,1)}, u32[]{:S(2)}) copy-start(bf16[8,768,128]{2,1,0:T(8,128)(2,1)} %get-tuple-element.34) | copy-start | bytes 4718596
  141.1 1.7 %copy-start.5 = (bf16[2,8,192,128]{3,2,1,0:T(8,128)(2,1)S(1)}, bf16[2,8,192,128]{3,2,1,0:T(8,128)(2,1)}, u32[]{:S(2)}) copy-start(bf16[2,8,192,128]{3,2,1,0:T(8,128)(2,1)} %get-tuple-element.35) | copy-start | bytes 2359300

commit v4 on v3

--- a/solution.py
+++ b/solution.py
@@ -205,9 +205,9 @@
     rows = out_ref.shape[1]
     tokens = kv_ref.shape[2]
     blk_copies = []
-    for d in range(1, peers):
-        peer = lax.rem(rank + d, peers)
-        for g in range(groups):
+    for g in range(groups):
+        for d in range(1, peers):
+            peer = lax.rem(rank + d, peers)
             copy = pltpu.make_async_remote_copy(
                 src_ref=far_refs[g].at[peer], dst_ref=recv.at[rank, g],
                 send_sem=blk_send.at[g, d], recv_sem=blk_recv.at[g, d],
@@ -223,7 +223,8 @@
         for g in range(1, groups):
             pairs.append((last_refs[g - 1].at[0, here], out_ref.at[me * groups + g]))
             pairs.append((last_refs[g - 1].at[1, here], dq_ref.at[me * groups + g]))
-        pairs.append((stage.at[:, :, some], kv_ref.at[:, pl.ds(me * groups, groups)]))
+        for g in range(groups):
+            pairs.append((stage.at[:, g, some], kv_ref.at[:, me * groups + g]))
         return pairs
 
     copies = []
@@ -255,9 +256,9 @@
             )
             copy.start()
             copies.append(copy)
-    for copy in blk_copies:
-        copy.wait()
     for g in range(groups):
+        for copy in blk_copies[g * (peers - 1) : (g + 1) * (peers - 1)]:
+            copy.wait_recv()
         for n in range(2):
             def settle(i, _):
                 at = pl.ds(pl.multiple_of(i * BLOCK, BLOCK), BLOCK)
@@ -273,7 +274,9 @@
                 return 0
 
             lax.fori_loop(0, run_blocks, settle, 0)
-    send(last)
+        send(last + g)
+    for copy in blk_copies:
+        copy.wait_send()
     for copy in copies:
         copy.wait()
 
@@ -421,8 +424,8 @@
         scratch_shapes=[
             pltpu.VMEM((peers, groups, 2, BLOCK, width), bf16),
             pltpu.VMEM(own_shape, bf16),
-            dma((2 * groups - 1,)), dma((2, heads)),
-            dma((2 * groups - 1, heads)), dma((2 * groups - 1, heads)),
+            dma((3 * groups - 2,)), dma((2, heads)),
+            dma((3 * groups - 2, heads)), dma((3 * groups - 2, heads)),
             dma((groups, peers)), dma((groups, peers)),
         ],
         compiler_params=params(collective_id=1),

time: 145 us -> 139 us (0.959)
  Pallas kernels: 119 us -> 113 us
    pallas_call x1, Pallas kernels: 41.5 us -> 35.3 us  [on_device(): pl.pallas_call(functools.partial(return_kernel, heads, peers, groups, run...]
  transfers between devices with their start and end apart: 6 -> 6, of which waited for: 0 -> 0; matrix products, arithmetic and copies ran while one was open for 3% -> 3% of each run, Pallas kernels for 26% -> 27%
where the time goes in v4:
time: 139 us
  Pallas kernels  113 us (81%)
  local copies, waits for them, and re-layouts  19.1 us (14%)
  starting transfers between devices  4.06 us (3%)
  other arithmetic  1.74 us (1%)
    pallas_call x1, Pallas kernels, on_device(): pl.pallas_call(functools.partial(bring_kernel, heads, peers, groups, run_...  40.4 us
    pallas_call x2, Pallas kernels, attend(): pl.pallas_call(functools.partial(attend_kernel, group, groups, run_blocks...  37.1 us
    pallas_call x1, Pallas kernels, on_device(): pl.pallas_call(functools.partial(return_kernel, heads, peers, groups, run...  35.3 us
    unnamed x29, local copies, waits for them, and re-layouts  5.9 us
    transpose x2, local copies, waits for them, and re-layouts, by_token(): jnp.transpose(array, (1, 0, 2, 3))  4.89 us
  transfers between devices with their start and end apart: 6, of which 0 were waited for; matrix products, arithmetic and copies ran while one was open for 3% of the time, Pallas kernels for 27%

profile of v4, /device:TPU:13, one launch (start us, length us, event | category | flops | bytes accessed | tf_op | source)
XLA Modules:
  0.0 138.7 jit_solution(17158278142187216711)
XLA Ops:
  0.7 2.1 %copy.18 = bf16[192,8,4,128]{3,2,0,1:T(4,128)(2,1)S(1)} copy(bf16[192,8,4,128]{3,2,1,0:T(4,128)(2,1)} %bitcast.46) | data formatting | bytes 3145728 | tf_op jit(solution)/shard_map/reshape | solution.py:298
  2.8 0.5 copy.19
  3.5 0.8 select_reduce_fusion
  4.5 0.7 reshape.63.named
  5.4 0.8 copy-done.9
  6.3 1.0 copy_bitcast_fusion
  7.3 40.4 %bring.1 = (bf16[3072,128]{1,0:T(8,128)(2,1)}, bf16[3072,128]{1,0:T(8,128)(2,1)}, bf16[2,2,768,128]{3,2,1,0:T(8,128)(2,1)}, bf16[8,2,2,128,128]{4,3,2,1,0:T(8,128)(2,1)}) custom-call(s32[16]{0:T(128)} %reshape.63.named, bf16[8,768,128]{2,1,0:T(8,128)(2,1)} %bitcast.43, bf16[8,768,128]{2,1,0:T(8,128)(2,1)} %bitcast.45, ...), custom_call_target="tpu_custom_call" | custom-call | tf_op jit(solution)/shard_map/bring/pallas_call | solution.py:317
  47.8 0.5 collective-permute-start.3
  48.3 1.3 collective-permute-start.4
  49.9 0.7 reshape.64.lists
  50.6 0.7 pad_add_fusion.place
  51.3 18.5 %attend_0.1 = (bf16[2,3072,128]{2,1,0:T(8,128)(2,1)}, bf16[2,768,128]{2,1,0:T(8,128)(2,1)}, bf16[8,2,128,128]{3,2,1,0:T(8,128)(2,1)}) custom-call(s32[2]{0:T(128)} %pad_add_fusion.place, s32[3072]{0:T(1024)} %reshape.64.lists, bf16[3072,128]{1,0:T(8,128)(2,1)} %get-tuple-element.20.q_ref, bf16[3072,128]{1,0:T(8,128)(2,1)} %get-tuple-element.21.do_ref, ...), custom_call_target="tpu_custom_call" | custom-call | flops 4831838208 | bytes 3145728 | tf_op jit(solution)/shard_map/attend_0/pallas_call | solution.py:359
  69.8 2.5 %constant_dynamic-slice_fusion.8 = (bf16[2,768,128]{2,1,0:T(8,128)(2,1)}, bf16[2,768,128]{2,1,0:T(8,128)(2,1)}, bf16[2,768,128]{2,1,0:T(8,128)(2,1)}, bf16[2,768,128]{2,1,0:T(8,128)(2,1)}) fusion(bf16[2,3072,128]{2,1,0:T(8,128)(2,1)} %get-tuple-element.24, s32[]{:T(128)S(6)} %select_n.55, s32[]{:T(128)S(6)} %select_n.54, s32[]{:T(128)S(6)} %select_n.53, ...), kind=kLoop, calls=%fused_computation.25 | loop fusion | bytes 3145744 | tf_op jit(solution)/shard_map/dynamic_slice | solution.py:408
  72.3 1.7 %collective-permute-start = (bf16[2,768,128]{2,1,0:T(8,128)(2,1)}, bf16[2,768,128]{2,1,0:T(8,128)(2,1)S(1)}, u32[]{:S(2)}, u32[]{:S(2)}) collective-permute-start(bf16[2,768,128]{2,1,0:T(8,128)(2,1)} %get-tuple-element.54), channel_id=1, source_target_pairs={{0,8},{8,16},{16,24},{24,0},{1,9},{9,17},{17,25},{25,1},{2,10},{10... | collective-permute-start | bytes 1179656 | tf_op jit(solution)/shard_map/ppermute | solution.py:409
  74.5 0.7 copy-done.11
  75.3 0.2 collective-permute-start.2
  75.7 1.1 copy-done.4
  76.8 18.5 %attend_1.1 = (bf16[2,3072,128]{2,1,0:T(8,128)(2,1)}, bf16[2,768,128]{2,1,0:T(8,128)(2,1)}, bf16[8,2,128,128]{3,2,1,0:T(8,128)(2,1)}) custom-call(s32[2]{0:T(128)} %pad_add_fusion.place, s32[3072]{0:T(1024)} %reshape.64.lists, bf16[2,3072,128]{2,1,0:T(8,128)(2,1)} %copy-done.4, bf16[2,3072,128]{2,1,0:T(8,128)(2,1)} %copy-done.4, ...), custom_call_target="tpu_custom_call" | custom-call | flops 4831838208 | bytes 3145728 | tf_op jit(solution)/shard_map/attend_1/pallas_call | solution.py:359
  95.5 0.7 copy-done.6
  96.4 35.3 %give_back.1 = (bf16[8,768,128]{2,1,0:T(8,128)(2,1)}, bf16[8,768,128]{2,1,0:T(8,128)(2,1)}, bf16[2,8,192,128]{3,2,1,0:T(8,128)(2,1)}) custom-call(s32[16]{0:T(128)} %reshape.63.named, bf16[2,768,128]{2,1,0:T(8,128)(2,1)} %get-tuple-element.55.refs_0_, bf16[2,768,128]{2,1,0:T(8,128)(2,1)} %copy-done.6, bf16[2,768,128]{2,1,0:T(8,128)(2,1)} %copy-done.7, ...), custom_call_target="tpu_custom_call" | custom-call | tf_op jit(solution)/shard_map/give_back/pallas_call | solution.py:411
  131.8 3.2 %copy.22 = bf16[192,8,4,128]{3,2,1,0:T(4,128)(2,1)} copy(bf16[192,8,4,128]{3,2,0,1:T(4,128)(2,1)} %bitcast.51) | data formatting | bytes 3145728 | tf_op jit(solution)/shard_map/transpose | solution.py:443
  135.0 1.7 %copy.23 = bf16[192,8,4,128]{3,2,1,0:T(4,128)(2,1)} copy(bf16[192,8,4,128]{3,2,0,1:T(4,128)(2,1)S(1)} %bitcast.50) | data formatting | bytes 3145728 | tf_op jit(solution)/shard_map/transpose | solution.py:443
  136.7 1.0 copy.24
  137.7 1.0 copy.25
  (46 shorter events, 1.9 us)
Async XLA Ops:
  0.7 2.1 %copy-start.2 = (bf16[192,32,128]{2,1,0:T(8,128)(2,1)S(1)}, bf16[192,32,128]{2,1,0:T(8,128)(2,1)}, u32[]{:S(2)}) copy-start(bf16[192,32,128]{2,1,0:T(8,128)(2,1)} %param.9) | copy-start | bytes 4718596
  2.8 2.4 %copy-start = (bf16[192,8,4,128]{3,2,0,1:T(4,128)(2,1)}, bf16[192,8,4,128]{3,2,0,1:T(4,128)(2,1)S(1)}, u32[]{:S(2)}) copy-start(bf16[192,8,4,128]{3,2,0,1:T(4,128)(2,1)S(1)} %copy.18) | copy-start | bytes 4718596
  3.3 2.0 %copy-start.1 = (bf16[192,8,4,128]{3,2,0,1:T(4,128)(2,1)}, bf16[192,8,4,128]{3,2,0,1:T(4,128)(2,1)S(1)}, u32[]{:S(2)}) copy-start(bf16[192,8,4,128]{3,2,0,1:T(4,128)(2,1)S(1)} %copy.19) | copy-start | bytes 4718596
  5.2 1.0 copy-start.9
  5.2 1.1 copy-start.10
  47.7 2.0 %copy-start.12 = (s32[8,48,8]{1,2,0:T(8,128)S(1)}, s32[8,48,8]{1,2,0:T(8,128)}, u32[]{:S(2)}) copy-start(s32[8,48,8]{1,2,0:T(8,128)} %param.8) | copy-start | bytes 36868
  47.8 26.8 %collective-permute-start.3 = (bf16[2,768,128]{2,1,0:T(8,128)(2,1)S(1)}, bf16[2,768,128]{2,1,0:T(8,128)(2,1)S(1)}, u32[]{:S(2)}, u32[]{:S(2)}) collective-permute-start(bf16[2,768,128]{2,1,0:T(8,128)(2,1)S(1)} %pad_maximum_fusion), channel_id=1, source_target_pairs={{0,8},{8,16},{16,24},{24,0},{1,9},{9,17},{17,25},{25,1},{2,10},{10... | collective-permute-start | bytes 1179656 | tf_op jit(solution)/shard_map/ppermute | solution.py:350
  48.3 27.2 %collective-permute-start.4 = (bf16[2,768,128]{2,1,0:T(8,128)(2,1)S(1)}, bf16[2,768,128]{2,1,0:T(8,128)(2,1)S(1)}, u32[]{:S(2)}, u32[]{:S(2)}) collective-permute-start(bf16[2,768,128]{2,1,0:T(8,128)(2,1)S(1)} %pad_maximum_fusion.1), channel_id=1, source_target_pairs={{0,16},{8,24},{16,0},{24,8},{1,17},{9,25},{17,1},{25,9},{2,18},{10... | collective-permute-start | bytes 1179656 | tf_op jit(solution)/shard_map/ppermute | solution.py:350
  49.7 25.9 %collective-permute-start.5 = (bf16[2,768,128]{2,1,0:T(8,128)(2,1)S(1)}, bf16[2,768,128]{2,1,0:T(8,128)(2,1)S(1)}, u32[]{:S(2)}, u32[]{:S(2)}) collective-permute-start(bf16[2,768,128]{2,1,0:T(8,128)(2,1)S(1)} %pad_maximum_fusion.2), channel_id=1, source_target_pairs={{0,24},{8,0},{16,8},{24,16},{1,25},{9,1},{17,9},{25,17},{2,26},{10... | collective-permute-start | bytes 1179656 | tf_op jit(solution)/shard_map/ppermute | solution.py:350
  72.3 23.0 %collective-permute-start = (bf16[2,768,128]{2,1,0:T(8,128)(2,1)}, bf16[2,768,128]{2,1,0:T(8,128)(2,1)S(1)}, u32[]{:S(2)}, u32[]{:S(2)}) collective-permute-start(bf16[2,768,128]{2,1,0:T(8,128)(2,1)} %get-tuple-element.54), channel_id=1, source_target_pairs={{0,8},{8,16},{16,24},{24,0},{1,9},{9,17},{17,25},{25,1},{2,10},{10... | collective-permute-start | bytes 1179656 | tf_op jit(solution)/shard_map/ppermute | solution.py:409
  74.1 21.3 %collective-permute-start.1 = (bf16[2,768,128]{2,1,0:T(8,128)(2,1)}, bf16[2,768,128]{2,1,0:T(8,128)(2,1)S(1)}, u32[]{:S(2)}, u32[]{:S(2)}) collective-permute-start(bf16[2,768,128]{2,1,0:T(8,128)(2,1)} %get-tuple-element.53), channel_id=1, source_target_pairs={{0,16},{8,24},{16,0},{24,8},{1,17},{9,25},{17,1},{25,9},{2,18},{10... | collective-permute-start | bytes 1179656 | tf_op jit(solution)/shard_map/ppermute | solution.py:409
  74.3 1.0 copy-start.11
  75.3 20.2 %collective-permute-start.2 = (bf16[2,768,128]{2,1,0:T(8,128)(2,1)S(1)}, bf16[2,768,128]{2,1,0:T(8,128)(2,1)S(1)}, u32[]{:S(2)}, u32[]{:S(2)}) collective-permute-start(bf16[2,768,128]{2,1,0:T(8,128)(2,1)S(1)} %copy-done.11), channel_id=1, source_target_pairs={{0,24},{8,0},{16,8},{24,16},{1,25},{9,1},{17,9},{25,17},{2,26},{10... | collective-permute-start | bytes 1179656 | tf_op jit(solution)/shard_map/ppermute | solution.py:409
  75.7 1.1 copy-start.4
  95.4 0.7 copy-start.6
  95.4 0.9 copy-start.7
  95.4 1.0 copy-start.8
  131.8 3.2 %copy-start.3 = (bf16[8,768,128]{2,1,0:T(8,128)(2,1)S(1)}, bf16[8,768,128]{2,1,0:T(8,128)(2,1)}, u32[]{:S(2)}) copy-start(bf16[8,768,128]{2,1,0:T(8,128)(2,1)} %get-tuple-element.34) | copy-start | bytes 4718596
  135.0 1.7 %copy-start.5 = (bf16[2,8,192,128]{3,2,1,0:T(8,128)(2,1)S(1)}, bf16[2,8,192,128]{3,2,1,0:T(8,128)(2,1)}, u32[]{:S(2)}) copy-start(bf16[2,8,192,128]{3,2,1,0:T(8,128)(2,1)} %get-tuple-element.35) | copy-start | bytes 2359300

commit v5 on v4

--- a/solution.py
+++ b/solution.py
@@ -41,17 +41,19 @@
     rows = q_ref.shape[1]
 
     def pieces(dest):
-        part = pl.ds(dest * groups, groups)
-        return (
-            (k_ref.at[part], kv_ref.at[0, :, pl.ds(pl.multiple_of(me * tokens, 64), tokens)]),
-            (v_ref.at[part], kv_ref.at[1, :, pl.ds(pl.multiple_of(me * tokens, 64), tokens)]),
+        here = pl.ds(pl.multiple_of(me * tokens, 64), tokens)
+        pairs = []
+        for g in range(groups):
+            pairs.append((k_ref.at[dest * groups + g], kv_ref.at[0, g, here]))
+            pairs.append((v_ref.at[dest * groups + g], kv_ref.at[1, g, here]))
+        return pairs + [
             (q_ref.at[dest * groups], qh_ref.at[pl.ds(pl.multiple_of(me * rows, 128), rows)]),
             (do_ref.at[dest * groups], doh_ref.at[pl.ds(pl.multiple_of(me * rows, 128), rows)]),
-        )
+        ]
 
     remote = {}
     local = []
-    for n in range(4):
+    for n in range(2 * groups + 2):
         for d in range(1, heads):
             dest = lax.rem(me + d, heads)
             src, dst = pieces(dest)[n]
@@ -66,14 +68,14 @@
         copy = pltpu.make_async_copy(src, dst, own_sem.at[n])
         copy.start()
         local.append(copy)
-    for n in range(2):
-        local[n].wait()
-        for d in range(1, heads):
-            remote[n, d].wait_recv()
     blk_copies = []
-    for d in range(1, peers):
-        peer = lax.rem(rank + d, peers)
-        for g in range(groups):
+    for g in range(groups):
+        for n in (2 * g, 2 * g + 1):
+            local[n].wait()
+            for d in range(1, heads):
+                remote[n, d].wait_recv()
+        for d in range(1, peers):
+            peer = lax.rem(rank + d, peers)
             block = named[g * peers + peer]
             for n in range(2):
                 total = jnp.zeros((BLOCK, kv_ref.shape[-1]), jnp.float32)
@@ -82,14 +84,14 @@
                     piece = kv_ref[n, g, i * BLOCK : (i + 1) * BLOCK, :]
                     total = total + weight * piece.astype(jnp.float32)
                 stage[d, n, g] = total.astype(jnp.bfloat16)
-        copy = pltpu.make_async_remote_copy(
-            src_ref=stage.at[d], dst_ref=recv_ref.at[rank],
-            send_sem=blk_send.at[d], recv_sem=blk_recv.at[d],
-            device_id=(me, peer), device_id_type=MESH,
-        )
-        copy.start()
-        blk_copies.append(copy)
-    for n in range(2, 4):
+            copy = pltpu.make_async_remote_copy(
+                src_ref=stage.at[d, :, g], dst_ref=recv_ref.at[rank, :, g],
+                send_sem=blk_send.at[g, d], recv_sem=blk_recv.at[g, d],
+                device_id=(me, peer), device_id_type=MESH,
+            )
+            copy.start()
+            blk_copies.append(copy)
+    for n in range(2 * groups, 2 * groups + 2):
         local[n].wait()
         for d in range(1, heads):
             remote[n, d].wait_recv()
@@ -326,7 +328,8 @@
         out_specs=(any_space, any_space, vmem, any_space),
         scratch_shapes=[
             pltpu.VMEM(far_shape, bf16),
-            dma((4,)), dma((4, heads)), dma((4, heads)), dma((peers,)), dma((peers,)),
+            dma((2 * groups + 2,)), dma((2 * groups + 2, heads)), dma((2 * groups + 2, heads)),
+            dma((groups, peers)), dma((groups, peers)),
         ],
         compiler_params=params(collective_id=0),
         name="bring",

time: 139 us -> 138 us (level)
  Pallas kernels: 113 us -> 111 us
    pallas_call x1, Pallas kernels: 40.4 us -> 37.5 us  [on_device(): pl.pallas_call(functools.partial(bring_kernel, heads, peers, groups, run_...]
where the time goes in v5:
time: 138 us; the launch traced here: 137 us
  Pallas kernels  111 us (80%)
  local copies, waits for them, and re-layouts  19.1 us (14%)
  starting transfers between devices  4.06 us (3%)
  other arithmetic  1.74 us (1%)
    pallas_call x1, Pallas kernels, on_device(): pl.pallas_call(functools.partial(bring_kernel, heads, peers, groups, run_...  37.5 us
    pallas_call x2, Pallas kernels, attend(): pl.pallas_call(functools.partial(attend_kernel, group, groups, run_blocks...  37.1 us
    pallas_call x1, Pallas kernels, on_device(): pl.pallas_call(functools.partial(return_kernel, heads, peers, groups, run...  36.6 us
    unnamed x29, local copies, waits for them, and re-layouts  5.9 us
    transpose x2, local copies, waits for them, and re-layouts, by_token(): jnp.transpose(array, (1, 0, 2, 3))  4.89 us
  transfers between devices with their start and end apart: 6, of which 0 were waited for; matrix products, arithmetic and copies ran while one was open for 3% of the time, Pallas kernels for 27%

profile of v5, /device:TPU:13, one launch (start us, length us, event | category | flops | bytes accessed | tf_op | source)
XLA Modules:
  0.0 137.1 jit_solution(4171598770105584413)
XLA Ops:
  0.7 2.1 %copy.18 = bf16[192,8,4,128]{3,2,0,1:T(4,128)(2,1)S(1)} copy(bf16[192,8,4,128]{3,2,1,0:T(4,128)(2,1)} %bitcast.46) | data formatting | bytes 3145728 | tf_op jit(solution)/shard_map/reshape | solution.py:300
  2.8 0.5 copy.19
  3.5 0.8 select_reduce_fusion
  4.5 0.7 reshape.63.named
  5.4 0.8 copy-done.9
  6.3 1.0 copy_bitcast_fusion
  7.3 37.5 %bring.1 = (bf16[3072,128]{1,0:T(8,128)(2,1)}, bf16[3072,128]{1,0:T(8,128)(2,1)}, bf16[2,2,768,128]{3,2,1,0:T(8,128)(2,1)}, bf16[8,2,2,128,128]{4,3,2,1,0:T(8,128)(2,1)}) custom-call(s32[16]{0:T(128)} %reshape.63.named, bf16[8,768,128]{2,1,0:T(8,128)(2,1)} %bitcast.43, bf16[8,768,128]{2,1,0:T(8,128)(2,1)} %bitcast.45, ...), custom_call_target="tpu_custom_call" | custom-call | tf_op jit(solution)/shard_map/bring/pallas_call | solution.py:319
  44.9 0.5 collective-permute-start.3
  45.4 1.3 collective-permute-start.4
  47.0 0.7 reshape.64.lists
  47.7 0.7 pad_add_fusion.place
  48.4 18.5 %attend_0.1 = (bf16[2,3072,128]{2,1,0:T(8,128)(2,1)}, bf16[2,768,128]{2,1,0:T(8,128)(2,1)}, bf16[8,2,128,128]{3,2,1,0:T(8,128)(2,1)}) custom-call(s32[2]{0:T(128)} %pad_add_fusion.place, s32[3072]{0:T(1024)} %reshape.64.lists, bf16[3072,128]{1,0:T(8,128)(2,1)} %get-tuple-element.20.q_ref, bf16[3072,128]{1,0:T(8,128)(2,1)} %get-tuple-element.21.do_ref, ...), custom_call_target="tpu_custom_call" | custom-call | flops 4831838208 | bytes 3145728 | tf_op jit(solution)/shard_map/attend_0/pallas_call | solution.py:362
  66.9 2.5 %constant_dynamic-slice_fusion.8 = (bf16[2,768,128]{2,1,0:T(8,128)(2,1)}, bf16[2,768,128]{2,1,0:T(8,128)(2,1)}, bf16[2,768,128]{2,1,0:T(8,128)(2,1)}, bf16[2,768,128]{2,1,0:T(8,128)(2,1)}) fusion(bf16[2,3072,128]{2,1,0:T(8,128)(2,1)} %get-tuple-element.24, s32[]{:T(128)S(6)} %select_n.55, s32[]{:T(128)S(6)} %select_n.54, s32[]{:T(128)S(6)} %select_n.53, ...), kind=kLoop, calls=%fused_computation.25 | loop fusion | bytes 3145744 | tf_op jit(solution)/shard_map/dynamic_slice | solution.py:411
  69.5 1.7 %collective-permute-start = (bf16[2,768,128]{2,1,0:T(8,128)(2,1)}, bf16[2,768,128]{2,1,0:T(8,128)(2,1)S(1)}, u32[]{:S(2)}, u32[]{:S(2)}) collective-permute-start(bf16[2,768,128]{2,1,0:T(8,128)(2,1)} %get-tuple-element.54), channel_id=1, source_target_pairs={{0,8},{8,16},{16,24},{24,0},{1,9},{9,17},{17,25},{25,1},{2,10},{10... | collective-permute-start | bytes 1179656 | tf_op jit(solution)/shard_map/ppermute | solution.py:412
  71.6 0.7 copy-done.11
  72.4 0.2 collective-permute-start.2
  72.8 1.1 copy-done.4
  74.0 18.5 %attend_1.1 = (bf16[2,3072,128]{2,1,0:T(8,128)(2,1)}, bf16[2,768,128]{2,1,0:T(8,128)(2,1)}, bf16[8,2,128,128]{3,2,1,0:T(8,128)(2,1)}) custom-call(s32[2]{0:T(128)} %pad_add_fusion.place, s32[3072]{0:T(1024)} %reshape.64.lists, bf16[2,3072,128]{2,1,0:T(8,128)(2,1)} %copy-done.4, bf16[2,3072,128]{2,1,0:T(8,128)(2,1)} %copy-done.4, ...), custom_call_target="tpu_custom_call" | custom-call | flops 4831838208 | bytes 3145728 | tf_op jit(solution)/shard_map/attend_1/pallas_call | solution.py:362
  92.6 0.7 copy-done.6
  93.5 36.6 %give_back.1 = (bf16[8,768,128]{2,1,0:T(8,128)(2,1)}, bf16[8,768,128]{2,1,0:T(8,128)(2,1)}, bf16[2,8,192,128]{3,2,1,0:T(8,128)(2,1)}) custom-call(s32[16]{0:T(128)} %reshape.63.named, bf16[2,768,128]{2,1,0:T(8,128)(2,1)} %get-tuple-element.55.refs_0_, bf16[2,768,128]{2,1,0:T(8,128)(2,1)} %copy-done.6, bf16[2,768,128]{2,1,0:T(8,128)(2,1)} %copy-done.7, ...), custom_call_target="tpu_custom_call" | custom-call | tf_op jit(solution)/shard_map/give_back/pallas_call | solution.py:414
  130.1 3.2 %copy.22 = bf16[192,8,4,128]{3,2,1,0:T(4,128)(2,1)} copy(bf16[192,8,4,128]{3,2,0,1:T(4,128)(2,1)} %bitcast.51) | data formatting | bytes 3145728 | tf_op jit(solution)/shard_map/transpose | solution.py:446
  133.3 1.7 %copy.23 = bf16[192,8,4,128]{3,2,1,0:T(4,128)(2,1)} copy(bf16[192,8,4,128]{3,2,0,1:T(4,128)(2,1)S(1)} %bitcast.50) | data formatting | bytes 3145728 | tf_op jit(solution)/shard_map/transpose | solution.py:446
  135.1 1.0 copy.24
  136.1 1.0 copy.25
  (46 shorter events, 1.9 us)
Async XLA Ops:
  0.7 2.1 %copy-start.2 = (bf16[192,32,128]{2,1,0:T(8,128)(2,1)S(1)}, bf16[192,32,128]{2,1,0:T(8,128)(2,1)}, u32[]{:S(2)}) copy-start(bf16[192,32,128]{2,1,0:T(8,128)(2,1)} %param.9) | copy-start | bytes 4718596
  2.8 2.4 %copy-start = (bf16[192,8,4,128]{3,2,0,1:T(4,128)(2,1)}, bf16[192,8,4,128]{3,2,0,1:T(4,128)(2,1)S(1)}, u32[]{:S(2)}) copy-start(bf16[192,8,4,128]{3,2,0,1:T(4,128)(2,1)S(1)} %copy.18) | copy-start | bytes 4718596
  3.3 2.0 %copy-start.1 = (bf16[192,8,4,128]{3,2,0,1:T(4,128)(2,1)}, bf16[192,8,4,128]{3,2,0,1:T(4,128)(2,1)S(1)}, u32[]{:S(2)}) copy-start(bf16[192,8,4,128]{3,2,0,1:T(4,128)(2,1)S(1)} %copy.19) | copy-start | bytes 4718596
  5.2 1.0 copy-start.9
  5.2 1.1 copy-start.10
  44.8 2.0 %copy-start.12 = (s32[8,48,8]{1,2,0:T(8,128)S(1)}, s32[8,48,8]{1,2,0:T(8,128)}, u32[]{:S(2)}) copy-start(s32[8,48,8]{1,2,0:T(8,128)} %param.8) | copy-start | bytes 36868
  44.9 26.8 %collective-permute-start.3 = (bf16[2,768,128]{2,1,0:T(8,128)(2,1)S(1)}, bf16[2,768,128]{2,1,0:T(8,128)(2,1)S(1)}, u32[]{:S(2)}, u32[]{:S(2)}) collective-permute-start(bf16[2,768,128]{2,1,0:T(8,128)(2,1)S(1)} %pad_maximum_fusion), channel_id=1, source_target_pairs={{0,8},{8,16},{16,24},{24,0},{1,9},{9,17},{17,25},{25,1},{2,10},{10... | collective-permute-start | bytes 1179656 | tf_op jit(solution)/shard_map/ppermute | solution.py:353
  45.4 27.2 %collective-permute-start.4 = (bf16[2,768,128]{2,1,0:T(8,128)(2,1)S(1)}, bf16[2,768,128]{2,1,0:T(8,128)(2,1)S(1)}, u32[]{:S(2)}, u32[]{:S(2)}) collective-permute-start(bf16[2,768,128]{2,1,0:T(8,128)(2,1)S(1)} %pad_maximum_fusion.1), channel_id=1, source_target_pairs={{0,16},{8,24},{16,0},{24,8},{1,17},{9,25},{17,1},{25,9},{2,18},{10... | collective-permute-start | bytes 1179656 | tf_op jit(solution)/shard_map/ppermute | solution.py:353
  46.8 25.9 %collective-permute-start.5 = (bf16[2,768,128]{2,1,0:T(8,128)(2,1)S(1)}, bf16[2,768,128]{2,1,0:T(8,128)(2,1)S(1)}, u32[]{:S(2)}, u32[]{:S(2)}) collective-permute-start(bf16[2,768,128]{2,1,0:T(8,128)(2,1)S(1)} %pad_maximum_fusion.2), channel_id=1, source_target_pairs={{0,24},{8,0},{16,8},{24,16},{1,25},{9,1},{17,9},{25,17},{2,26},{10... | collective-permute-start | bytes 1179656 | tf_op jit(solution)/shard_map/ppermute | solution.py:353
  69.5 23.0 %collective-permute-start = (bf16[2,768,128]{2,1,0:T(8,128)(2,1)}, bf16[2,768,128]{2,1,0:T(8,128)(2,1)S(1)}, u32[]{:S(2)}, u32[]{:S(2)}) collective-permute-start(bf16[2,768,128]{2,1,0:T(8,128)(2,1)} %get-tuple-element.54), channel_id=1, source_target_pairs={{0,8},{8,16},{16,24},{24,0},{1,9},{9,17},{17,25},{25,1},{2,10},{10... | collective-permute-start | bytes 1179656 | tf_op jit(solution)/shard_map/ppermute | solution.py:412
  71.2 21.3 %collective-permute-start.1 = (bf16[2,768,128]{2,1,0:T(8,128)(2,1)}, bf16[2,768,128]{2,1,0:T(8,128)(2,1)S(1)}, u32[]{:S(2)}, u32[]{:S(2)}) collective-permute-start(bf16[2,768,128]{2,1,0:T(8,128)(2,1)} %get-tuple-element.53), channel_id=1, source_target_pairs={{0,16},{8,24},{16,0},{24,8},{1,17},{9,25},{17,1},{25,9},{2,18},{10... | collective-permute-start | bytes 1179656 | tf_op jit(solution)/shard_map/ppermute | solution.py:412
  71.4 1.0 copy-start.11
  72.4 20.2 %collective-permute-start.2 = (bf16[2,768,128]{2,1,0:T(8,128)(2,1)S(1)}, bf16[2,768,128]{2,1,0:T(8,128)(2,1)S(1)}, u32[]{:S(2)}, u32[]{:S(2)}) collective-permute-start(bf16[2,768,128]{2,1,0:T(8,128)(2,1)S(1)} %copy-done.11), channel_id=1, source_target_pairs={{0,24},{8,0},{16,8},{24,16},{1,25},{9,1},{17,9},{25,17},{2,26},{10... | collective-permute-start | bytes 1179656 | tf_op jit(solution)/shard_map/ppermute | solution.py:412
  72.8 1.1 copy-start.4
  92.5 0.7 copy-start.6
  92.5 0.9 copy-start.7
  92.5 1.0 copy-start.8
  130.1 3.2 %copy-start.3 = (bf16[8,768,128]{2,1,0:T(8,128)(2,1)S(1)}, bf16[8,768,128]{2,1,0:T(8,128)(2,1)}, u32[]{:S(2)}) copy-start(bf16[8,768,128]{2,1,0:T(8,128)(2,1)} %get-tuple-element.34) | copy-start | bytes 4718596
  133.3 1.7 %copy-start.5 = (bf16[2,8,192,128]{3,2,1,0:T(8,128)(2,1)S(1)}, bf16[2,8,192,128]{3,2,1,0:T(8,128)(2,1)}, u32[]{:S(2)}) copy-start(bf16[2,8,192,128]{3,2,1,0:T(8,128)(2,1)} %get-tuple-element.35) | copy-start | bytes 2359300
